TPU v7x, 512 devices: a whole 4x8x8 slice. The times are simulated.
512 devices in a mesh: freq: 16 (over z, core), src: 32 (over x, y).
Axes of the slice: x: 4, y: 8, z: 8, core: 2. Of those that a mesh axis runs over, the one named last changes fastest.
Arguments:
- data: bfloat16 [2, 16, 128, 98304], P(None, 'freq', None, 'src'), may hold values from -6 to 6
- recip: bfloat16 [2, 16, 128, 512], P(None, 'freq', None, 'src'), may hold values from -6 to 6
- gap: int32 [128, 512], P(None, 'src'), may hold values 0 or 1
- owner: int32 [32], replicated, may hold values from 0 to 31, as said below
- weights: bfloat16 [2, 16, 98304, 256], P(None, 'freq', 'src'), may hold values from -0.02734375 to 0.02734375
- start_row: int32 [16], P('freq'), may hold values from 0 to 480, as said below
- end_row: int32 [16], P('freq'), may hold values from 32 to 512, as said below
- recorded: bfloat16 [768, 256, 128], P('freq', 'src'), may hold values from -6 to 6
Outputs:
- primaries: bfloat16 [768, 256, 128], P('freq', 'src')
- filters: float32 [16, 27], P('freq')
Inputs may be any that keep to these rules, and one draw needn't show every extreme that they name: `owner`: a permutation: each block is named by exactly one src index. `start_row`: start of window i lies between i * 32 - 8 and i * 32, never before 0; window 1 starts exactly 8 early. `end_row`: end of window i lies between (i + 1) * 32 and (i + 1) * 32 + 8, never after 512; window 1 ends exactly 8 late.
All inputs are finite; a program needn't handle non-finite values. No bound on the sum of `gap` on one device may be relied on, other than what follows from the above.
Results may differ from a plain program's by a relative error of at most 0.001.
Values may be sent and summed in bfloat16 or wider, within the bound.
No kernel may reach another device: no remote copies, remote signals or barrier semaphores. Data moves between devices by JAX's collectives and lax.ppermute only.
A program may use at most 64 MiB of HBM per device.

v0:
```python
import math

import jax
import jax.numpy as jnp
from jax import lax
from jax.sharding import PartitionSpec as P

RECV = 128
NFFT = 512
F_LOW = 40
NEAR = 16
HALO = 8
LAGS_T = 9
LAGS_X = 3


def padded_2(array, sides, width):
    for axis, dim in sides:
        devices, length = (lax.axis_size(axis), array.shape[dim])
        up = [(i, (i + 1) % devices) for i in range(devices - 1)]
        down = [(j, i) for i, j in up]
        last = lax.slice_in_dim(array, length - width, length, axis=dim)
        leading = lax.slice_in_dim(array, 0, width, axis=dim)
        before = lax.ppermute(last, axis, up)
        after = lax.ppermute(leading, axis, down)
        array = jnp.concatenate([before, array, after], axis=dim)
    return array


def phase_tables(times, freqs):
    turns = (F_LOW + freqs)[None, :] * times[:, None] % NFFT
    angle = turns.astype(jnp.float32) * (2.0 * math.pi / NFFT)
    return (jnp.cos(angle), jnp.sin(angle))


def shifted_stack(masked, keep):
    lead = LAGS_T // 2
    side = LAGS_X // 2
    padded = jnp.pad(masked, ((lead, lead), (0, 0), (side, side)))
    height = masked.shape[0]
    width = masked.shape[2]
    pieces = [
        padded[LAGS_T - 1 - a : LAGS_T - 1 - a + height, :, LAGS_X - 1 - b : LAGS_X - 1 - b + width]
        for a in range(LAGS_T)
        for b in range(LAGS_X)
    ]
    return jnp.stack(pieces) * keep[None, :, None, None]


def solve_filter(gram, rhs, damping):
    count = gram.shape[0]
    centre = LAGS_T // 2 * LAGS_X + LAGS_X // 2
    unit = (jnp.arange(count) == centre).astype(jnp.float32)
    eye = jnp.eye(count, dtype=jnp.float32)
    factor = jnp.linalg.cholesky(gram + damping * eye)
    return jax.scipy.linalg.cho_solve((factor, True), rhs + damping * unit)


def body(data, recip, gap, owner, weights, start_row, end_row, recorded):
    hp = lax.Precision.HIGHEST
    src_here = lax.axis_index("src")
    freq_here = lax.axis_index("freq")
    src_count = lax.axis_size("src")
    freq_count = lax.axis_size("freq")
    nfreq_local = data.shape[1]
    total_freq = nfreq_local * freq_count
    total_out = weights.shape[3]
    out_local = total_out // src_count
    block_rows = recorded.shape[0] - 2 * HALO
    total_time = block_rows * freq_count
    scale = 1.0 / math.sqrt(total_freq)
    piece = lax.all_gather(recip, "src", axis=3, tiled=True)
    count = piece.shape[3] // NEAR
    select = (owner == src_here).astype(jnp.float32)
    split = piece.reshape(2, nfreq_local, RECV, count, NEAR).astype(jnp.float32)
    filled = jnp.einsum("cfrqn,q->cfrn", split, select)
    near = jnp.where((gap == 1)[None, None], filled.astype(jnp.bfloat16), data[..., :NEAR])
    panel = jnp.concatenate([near, data[..., NEAR:]], axis=3)
    real = jnp.einsum(
        "frk,fks->sfr", panel[0], weights[0], preferred_element_type=jnp.float32
    ) - jnp.einsum("frk,fks->sfr", panel[1], weights[1], preferred_element_type=jnp.float32)
    imag = jnp.einsum(
        "frk,fks->sfr", panel[0], weights[1], preferred_element_type=jnp.float32
    ) + jnp.einsum("frk,fks->sfr", panel[1], weights[0], preferred_element_type=jnp.float32)
    summed = lax.psum(jnp.stack([real, imag], axis=1), "src")
    local_pred = lax.dynamic_slice_in_dim(summed, src_here * out_local, out_local, 0)
    spread = lax.all_to_all(local_pred, "freq", split_axis=3, concat_axis=2, tiled=True)
    cosine, sine = phase_tables(
        jnp.arange(total_time, dtype=jnp.int32), jnp.arange(total_freq, dtype=jnp.int32)
    )
    series = (
        jnp.einsum("tf,sfr->tsr", cosine, spread[:, 0], precision=hp)
        - jnp.einsum("tf,sfr->tsr", sine, spread[:, 1], precision=hp)
    ) * scale
    block = lax.all_to_all(series, "freq", split_axis=0, concat_axis=2, tiled=True)
    ext = padded_2(block, (("freq", 0),), HALO)
    rows = freq_here * block_rows - HALO + jnp.arange(recorded.shape[0], dtype=jnp.int32)
    keep = ((rows >= start_row[0]) & (rows < end_row[0])).astype(jnp.float32)
    target = recorded.astype(jnp.float32) * keep[:, None, None]
    stack = shifted_stack(ext * keep[:, None, None], keep)
    flat = stack.reshape(stack.shape[0], -1)
    gram = jnp.dot(flat, flat.T, precision=hp)
    rhs = jnp.dot(flat, target.reshape(-1), precision=hp)
    gram, rhs = lax.psum((gram, rhs), "src")
    damping = float(recorded.shape[0] * total_out * RECV)
    filt = solve_filter(gram, rhs, damping)
    matched = jnp.einsum("u,uwsr->wsr", filt, stack, precision=hp)
    primaries = (target - matched).astype(jnp.bfloat16)
    return (primaries, filt[None, :])


def solution(mesh):
    placed = (
        P(None, "freq", None, "src"),
        P(None, "freq", None, "src"),
        P(None, "src"),
        P(),
        P(None, "freq", "src", None),
        P("freq"),
        P("freq"),
        P("freq", "src", None),
    )
    return jax.shard_map(
        body,
        mesh=mesh,
        in_specs=placed,
        out_specs=(P("freq", "src", None), P("freq", None)),
        check_vma=False,
    )
```

profile of v0, /device:TPU:64, one launch (start us, length us, event | category | flops | bytes accessed | tf_op | source)
XLA Modules:
  0.0 439.7 jit_solution(16565742471671505517)
XLA Ops:
  7.2 0.9 broadcast_compare_fusion
  8.2 40.0 %all_gather.3 = bf16[2,1,128,512]{2,3,1,0:T(8,128)(2,1)S(1)} all-gather(bf16[2,1,128,16]{2,3,1,0:T(8,128)(2,1)} %param.9), channel_id=1, replica_groups=mesh['freq'=16,'src'=32] {'src'}, dimensions={3}, use_global_device_ids=true | all-gather | bytes 270336 | tf_op jit(solution)/shard_map/all_gather | solution.py:72
  48.2 0.8 fusion.41
  49.2 2.0 slice.138
  51.2 0.9 fusion.99
  52.0 1.9 fusion.6
  55.3 0.7 pad_maximum_fusion.1
  56.1 155.9 %all-reduce.4.cloned.1.call-done = f32[256,2,1,128]{0,3,2,1:T(8,128)} async-done(((f32[256,2,1,128]{0,3,2,1:T(8,128)}), f32[256,2,1,128]{0,3,2,1:T(8,128)}) %all-reduce.4.cloned.1.call-update) | async-done | bytes 262160 | tf_op jit(solution)/shard_map/psum | solution.py:85
  212.0 1.0 constant_dynamic-slice_fusion
  213.7 1.0 reduce.6
  214.6 0.8 reshape.160
  215.4 7.8 %all-to-all-start = ((f32[16,1,128]{2,1,0:T(1,128)}), f32[16,1,128]{2,1,0:T(1,128)S(1)}, u32[]{:S(2)}, u32[]{:S(2)}) async-start(f32[16,1,128]{2,1,0:T(1,128)} %reshape.160), calls=%async_computation | async-start | bytes 16384 | tf_op jit(solution)/shard_map/all_to_all | solution.py:87
  223.2 6.1 %all-to-all-done = f32[16,1,128]{2,1,0:T(1,128)S(1)} async-done(((f32[16,1,128]{2,1,0:T(1,128)}), f32[16,1,128]{2,1,0:T(1,128)S(1)}, u32[]{:S(2)}, u32[]{:S(2)}) %all-to-all-start) | async-done | bytes 8224 | tf_op jit(solution)/shard_map/all_to_all | solution.py:87
  231.4 0.7 copy.50
  232.1 1.7 reshape.162
  233.8 4.9 %all-to-all-start.1 = ((f32[16,1,2048]{2,1,0:T(1,128)}), f32[16,1,2048]{2,1,0:T(1,128)S(1)}, u32[]{:S(2)}, u32[]{:S(2)}) async-start(f32[16,1,2048]{2,1,0:T(1,128)} %reshape.162), calls=%async_computation.1 | async-start | bytes 262144 | tf_op jit(solution)/shard_map/all_to_all | solution.py:95
  240.0 6.3 %all-to-all-done.1 = f32[16,1,2048]{2,1,0:T(1,128)S(1)} async-done(((f32[16,1,2048]{2,1,0:T(1,128)}), f32[16,1,2048]{2,1,0:T(1,128)S(1)}, u32[]{:S(2)}, u32[]{:S(2)}) %all-to-all-start.1) | async-done | bytes 131104 | tf_op jit(solution)/shard_map/all_to_all | solution.py:95
  246.3 0.9 reduce.8
  247.2 1.1 reshape.163
  248.3 0.7 copy.51
  249.6 3.7 collective-permute-start.1
  253.3 2.1 collective-permute-start
  255.8 2.7 collective-permute-done
  261.0 0.8 broadcast_multiply_fusion
  261.8 7.2 %fusion.32 = f32[27,27]{1,0:T(8,128)S(1)} fusion(f32[27,48,8,128]{3,2,1,0:T(8,128)S(1)} %broadcast_multiply_fusion), kind=kOutput, calls=%fused_computation.55 | convolution fusion | flops 429981696 | bytes 5311332 | tf_op jit(solution)/shard_map/dot_general | solution.py:102
  269.0 7.6 %fusion.35 = f32[27]{0:T(128)S(1)} fusion(f32[48,8,128,1]{2,3,1,0:T(1,128)S(1)} %bitcast.242, f32[27,48,8,128]{3,2,1,0:T(8,128)S(1)} %broadcast_multiply_fusion), kind=kOutput, calls=%fused_computation.57 | convolution fusion | flops 15925248 | bytes 5505132 | tf_op jit(solution)/shard_map/dot_general | solution.py:103
  276.6 140.5 %all-reduce.1 = (f32[27,27]{1,0:T(8,128)S(1)}, f32[27]{0:T(128)S(1)}) all-reduce(f32[27,27]{1,0:T(8,128)S(1)} %fusion.32, f32[27]{0:T(128)S(1)} %fusion.35), channel_id=1, replica_groups=mesh['freq'=16,'src'=32] {'src'}, use_global_device_ids=true, to_apply=%region_1.2 | all-reduce | flops 756 | bytes 6048 | tf_op jit(solution)/shard_map/psum | solution.py:104
  417.2 2.5 cholesky.16
  420.3 0.7 fusion.110
  421.0 2.1 custom-call.10
  423.3 8.7 %fusion = f32[1,48,8,128]{3,0,2,1:T(1,128)S(1)} fusion(f32[27,48,8,128]{3,2,1,0:T(8,128)} %copy-done, f32[1,27]{1,0:T(1,128)S(1)} %fusion.111), kind=kOutput, calls=%fused_computation | convolution fusion | flops 15925248 | bytes 5505132 | tf_op jit(solution)/shard_map/u,uwsr->wsr/dot_general | solution.py:107
  432.1 0.8 subtract_convert_fusion
  (67 shorter events, 8.7 us)
Async XLA Ops:
  7.2 46.8 %copy-start.3 = (bf16[2,1,3072,256]{3,2,1,0:T(8,128)(2,1)S(1)}, bf16[2,1,3072,256]{3,2,1,0:T(8,128)(2,1)}, u32[]{:S(2)}) copy-start(bf16[2,1,3072,256]{3,2,1,0:T(8,128)(2,1)} %param.12) | copy-start | bytes 9437188
  7.2 204.8 %all-reduce.4.cloned.1.call-start = ((), (), s32[]{:S(2)}) async-start(), calls=%async_computation.2 | async-start | bytes 524288 | tf_op jit(solution)/shard_map/psum | solution.py:85
  215.4 13.9 %all-to-all-start = ((f32[16,1,128]{2,1,0:T(1,128)}), f32[16,1,128]{2,1,0:T(1,128)S(1)}, u32[]{:S(2)}, u32[]{:S(2)}) async-start(f32[16,1,128]{2,1,0:T(1,128)} %reshape.160), calls=%async_computation | async-start | bytes 16384 | tf_op jit(solution)/shard_map/all_to_all | solution.py:87
  233.8 24.7 %copy-start.1 = (bf16[48,8,128]{2,1,0:T(8,128)(2,1)S(1)}, bf16[48,8,128]{2,1,0:T(8,128)(2,1)}, u32[]{:S(2)}) copy-start(bf16[48,8,128]{2,1,0:T(8,128)(2,1)} %param.15) | copy-start | bytes 294916
  233.8 12.5 %all-to-all-start.1 = ((f32[16,1,2048]{2,1,0:T(1,128)}), f32[16,1,2048]{2,1,0:T(1,128)S(1)}, u32[]{:S(2)}, u32[]{:S(2)}) async-start(f32[16,1,2048]{2,1,0:T(1,128)} %reshape.162), calls=%async_computation.1 | async-start | bytes 262144 | tf_op jit(solution)/shard_map/all_to_all | solution.py:95
  249.6 6.2 %collective-permute-start.1 = (f32[8,8,128]{2,1,0:T(8,128)S(1)}, f32[8,8,128]{2,1,0:T(8,128)S(1)}, u32[]{:S(2)}, u32[]{:S(2)}) collective-permute-start(f32[8,8,128]{2,1,0:T(8,128)S(1)} %copy.71), channel_id=1, source_target_pairs={{32,0},{64,32},{96,64},{128,96},{160,128},{192,160},{224,192},{256... | collective-permute-start | bytes 98312 | tf_op jit(solution)/shard_map/ppermute | solution.py:25
  253.3 5.2 %collective-permute-start = (f32[8,8,128]{2,1,0:T(8,128)S(1)}, f32[8,8,128]{2,1,0:T(8,128)S(1)}, u32[]{:S(2)}, u32[]{:S(2)}) collective-permute-start(f32[8,8,128]{2,1,0:T(8,128)S(1)} %copy.70), channel_id=1, source_target_pairs={{0,32},{32,64},{64,96},{96,128},{128,160},{160,192},{192,224},{224... | collective-permute-start | bytes 98312 | tf_op jit(solution)/shard_map/ppermute | solution.py:24
  261.8 7.2 %copy-start = (f32[27,48,8,128]{3,2,1,0:T(8,128)}, f32[27,48,8,128]{3,2,1,0:T(8,128)S(1)}, u32[]{:S(2)}) copy-start(f32[27,48,8,128]{3,2,1,0:T(8,128)S(1)} %broadcast_multiply_fusion) | copy-start | bytes 15925252
  423.3 9.5 %copy-start.2 = (f32[1,27]{1,0:T(1,128)}, f32[1,27]{1,0:T(1,128)S(1)}, u32[]{:S(2)}) copy-start(f32[1,27]{1,0:T(1,128)S(1)} %fusion.111) | copy-start | bytes 328
Sparse Core Ops, SparseCore 0:
  56.2 155.7 all-reduce.3
where the time goes:
time: 440 us
  blocking collectives  181 us (41%)
  waiting for transfers between devices  171 us (39%)
  matrix products  28.7 us (7%)
  starting transfers between devices  18.5 us (4%)
  between operations  15.8 us (4%)
  local copies, waits for them, and re-layouts  12.6 us (3%)
  other arithmetic  12.5 us (3%)
    psum x1, waiting for transfers between devices, body(): summed = lax.psum(jnp.stack([real, imag], axis=1), 'src')  156 us
    psum x1, blocking collectives, body(): gram, rhs = lax.psum((gram, rhs), 'src')  140 us
    all_gather x1, blocking collectives, body(): piece = lax.all_gather(recip, 'src', axis=3, tiled=True)  40 us
  transfers between devices with their start and end apart: 5, of which 4 were waited for; matrix products, arithmetic and copies ran while one was open for 0% of the time, Pallas kernels for 0%

commit v1 on v0

v1 whole, which is shorter than its diff:
```python
import functools
import math

import jax
import jax.numpy as jnp
import ml_dtypes
import numpy as np
from jax import lax
from jax.experimental import pallas as pl
from jax.experimental.pallas import tpu as pltpu
from jax.sharding import PartitionSpec as P

RECV = 128
NFFT = 512
F_LOW = 40
NEAR = 16
HALO = 8
LAGS_T = 9
LAGS_X = 3
LEAD = LAGS_T // 2
T_DEV = 32
WROWS = T_DEV + 2 * HALO
NF = 16
GROUP = 4
GROWS = 256
SIDE = 40
TARGET_COL = GROUP * LEAD + 3
CENTRE_ROW = GROUP * LEAD + 1
PACK_AT = (0, 40, 72, 96, 112)
VMEM = pl.BlockSpec(memory_space=pltpu.VMEM)
SMEM = pl.BlockSpec(memory_space=pltpu.SMEM)
F32 = jnp.float32
BF16 = jnp.bfloat16


def split3(x):
    high = x.astype(ml_dtypes.bfloat16)
    rest = x - high.astype(np.float32)
    mid = rest.astype(ml_dtypes.bfloat16)
    low = (rest - mid.astype(np.float32)).astype(ml_dtypes.bfloat16)
    return high, mid, low


@functools.cache
def phase_rows():
    table = np.zeros((NF, GROWS, 256), ml_dtypes.bfloat16)
    freqs = np.arange(NF)
    scale = 1.0 / math.sqrt(NF)
    for window in range(NF):
        for row in range(WROWS):
            time = window * T_DEV - HALO + row
            if not 0 <= time < NFFT:
                continue
            turns = (F_LOW + freqs) * time % NFFT
            angle = turns * (2.0 * math.pi / NFFT)
            phase = np.stack([np.cos(angle), -np.sin(angle)], axis=1).reshape(-1) * scale
            high, mid, low = split3(phase.astype(np.float32))
            at = GROUP * (row + LEAD)
            table[window, at : at + 3, :192] = np.concatenate([high, high, mid, high, low, mid])
            table[window, at + 3, 192 + row] = 1
    return table


def main_product(mask_ref, data_ref, weights_ref, out_ref, acc_ref):
    step = pl.program_id(0)
    depth = data_ref.shape[3]

    @pl.when(step == 0)
    def _():
        acc_ref[...] = jnp.zeros_like(acc_ref)

    panel = data_ref[...].reshape(2 * RECV, depth)
    mask = jnp.where(step == 0, mask_ref[...], jnp.ones_like(mask_ref))
    near = panel[:, :RECV] * jnp.concatenate([mask, mask], axis=0)
    panel = jnp.concatenate([near, panel[:, RECV:]], axis=1)
    both = jnp.concatenate([weights_ref[0, 0], weights_ref[1, 0]], axis=1)
    product = jnp.dot(panel, both, preferred_element_type=F32)
    half = product.shape[1] // 2
    acc_ref[0] += product[:RECV, :half] - product[RECV:, half:]
    acc_ref[1] += product[:RECV, half:] + product[RECV:, :half]

    @pl.when(step == pl.num_programs(0) - 1)
    def _():
        out_ref[0] = acc_ref[0].T
        out_ref[1] = acc_ref[1].T


def add_fill(pred_ref, recip_ref, gap_ref, near_ref, out_ref):
    slots = out_ref.shape[0]
    piece = jnp.sum(recip_ref[...].astype(F32), axis=0).astype(BF16)
    fill = jnp.dot(near_ref[...], piece * gap_ref[...], preferred_element_type=F32)
    total = pred_ref[...].reshape(fill.shape) + fill
    half = slots * 8
    out_ref[:, :8, :] = total[:half].reshape(slots, 8, RECV)
    out_ref[:, 8:, :] = total[half:].reshape(slots, 8, RECV)


def sum_slots(part_ref, out_ref):
    total = jnp.sum(part_ref[...], axis=0)
    out_ref[...] = jnp.broadcast_to(total[None], out_ref.shape)


def two_parts(x):
    high = x.astype(BF16)
    return high, (x - high.astype(F32)).astype(BF16)


def trace_and_gram(lohi_ref, x_ref, rows_ref, target_ref, gram_ref, trace_ref, a_ref, g_ref):
    sources = 8
    x = jnp.concatenate([x_ref[pl.ds(s, 2 * NF, stride=sources), :] for s in range(sources)], axis=1)
    high, rest = x.astype(BF16), x
    rest = rest - high.astype(F32)
    mid = rest.astype(BF16)
    low = (rest - mid.astype(F32)).astype(BF16)
    stack = jnp.concatenate([high, mid, high, low, high, mid, target_ref[...]], axis=0)
    base = jnp.dot(rows_ref[...], stack, preferred_element_type=F32)
    lag = lax.rem(lax.broadcasted_iota(jnp.int32, (GROWS, RECV), 0), GROUP)
    recv = lax.broadcasted_iota(jnp.int32, (GROWS, RECV), 1)
    ahead = (lag == 0) & (recv < RECV - 1)
    behind = (lag == 2) & (recv > 0)
    same = (lag == 1) | (lag == 3)
    for s in range(sources):
        at = slice(s * RECV, (s + 1) * RECV)
        here = base[:, at]
        shifted = jnp.where(
            same,
            here,
            jnp.where(
                ahead,
                pltpu.roll(here, RECV - 1, 1),
                jnp.where(behind, pltpu.roll(here, 1, 1), 0.0),
            ),
        )
        a_ref[s * GROWS : (s + 1) * GROWS, :] = shifted
    for s in range(sources):
        mine = a_ref[pl.ds(s * GROWS + 1, WROWS + 2 * LEAD, stride=GROUP), :]
        trace_ref[pl.ds(s, WROWS + 2 * LEAD, stride=sources), :] = mine
    high, low = two_parts(jnp.concatenate([a_ref[s * GROWS : (s + 1) * GROWS, :] for s in range(sources)], axis=1))
    dims = (((1,), (1,)), ((), ()))
    g_ref[...] = lax.dot_general(high, high, dims, preferred_element_type=F32) + 2.0 * lax.dot_general(
        high, low, dims, preferred_element_type=F32
    )
    first, last = lohi_ref[0], lohi_ref[1]
    total = jnp.zeros((SIDE, RECV), F32)
    for u in range(WROWS):
        at = GROUP * u
        if at + SIDE <= RECV:
            part = g_ref[at : at + SIDE, :RECV]
            part = pltpu.roll(part, (RECV - at) % RECV, 1)
        elif at >= RECV:
            part = g_ref[at : at + SIDE, RECV:]
            part = pltpu.roll(part, (2 * RECV - at) % RECV, 1)
        else:
            part = pltpu.roll(g_ref[at : at + SIDE, :], 2 * RECV - at, 1)[:, :RECV]
        kept = jnp.where((u >= first) & (u < last), 1.0, 0.0)
        total = total + part * kept
    full = jnp.concatenate([total, jnp.zeros((RECV - SIDE, RECV), F32)], axis=0)
    total = 0.5 * (total + full.T[:SIDE])
    lanes = lax.broadcasted_iota(jnp.int32, (8, RECV), 1)
    packed = jnp.zeros((8, RECV), F32)
    for g, at in enumerate(PACK_AT):
        piece = total[8 * g : 8 * g + 8]
        piece = jnp.where((lanes >= 8 * g) & (lanes < SIDE), piece, 0.0)
        packed = packed + pltpu.roll(piece, at - 8 * g, 1)
    gram_ref[...] = jnp.broadcast_to(packed[None], gram_ref.shape)


def solve_and_filter(damping, lohi_ref, gram_ref, trace_ref, recorded_ref, out_ref, filters_ref, h_ref):
    packed = jnp.sum(gram_ref[...], axis=0)
    lanes = lax.broadcasted_iota(jnp.int32, (8, RECV), 1)
    pieces = []
    for g, at in enumerate(PACK_AT):
        piece = pltpu.roll(packed, (RECV + 8 * g - at) % RECV, 1)
        pieces.append(jnp.where((lanes >= 8 * g) & (lanes < SIDE), piece, 0.0))
    upper = jnp.concatenate(pieces, axis=0)
    full = jnp.concatenate([upper, jnp.zeros((RECV - SIDE, RECV), F32)], axis=0)
    row = lax.broadcasted_iota(jnp.int32, (SIDE, RECV), 0)
    lane = lax.broadcasted_iota(jnp.int32, (SIDE, RECV), 1)
    system = jnp.where(lane // 8 < row // 8, full.T[:SIDE], upper)
    unknown = lax.rem(row, GROUP) < LAGS_X
    system = system + jnp.where((row == lane) & unknown, damping, 0.0)
    system = system + jnp.where((row == CENTRE_ROW) & (lane == TARGET_COL), damping, 0.0)
    for k in range(GROUP * LAGS_T):
        if k % GROUP >= LAGS_X:
            continue
        pivot_row = system[k : k + 1, :]
        column = jnp.broadcast_to(system[:, k : k + 1], (SIDE, RECV))
        scaled = pivot_row / jnp.broadcast_to(system[k : k + 1, k : k + 1], (1, RECV))
        system = jnp.where(row == k, scaled, system - column * scaled)
    h_ref[...] = jnp.broadcast_to(system[:, TARGET_COL : TARGET_COL + 1], (SIDE, RECV))
    filters_ref[...] = h_ref[...]
    first, last = lohi_ref[0], lohi_ref[1]
    recv = lax.broadcasted_iota(jnp.int32, (8, RECV), 1)
    taps = [[jnp.broadcast_to(h_ref[GROUP * p + c : GROUP * p + c + 1, :], (8, RECV)) for c in range(LAGS_X)] for p in range(LAGS_T)]
    for u in range(WROWS):
        sums = [None] * LAGS_X
        for p in range(LAGS_T):
            value = trace_ref[8 * (u + p) : 8 * (u + p) + 8, :]
            for c in range(LAGS_X):
                term = taps[p][c] * value
                sums[c] = term if sums[c] is None else sums[c] + term
        ahead = jnp.where(recv < RECV - 1, pltpu.roll(sums[0], RECV - 1, 1), 0.0)
        behind = jnp.where(recv > 0, pltpu.roll(sums[2], 1, 1), 0.0)
        kept = jnp.where((u >= first) & (u < last), 1.0, 0.0)
        value = recorded_ref[u].astype(F32) - (sums[1] + ahead + behind)
        out_ref[u] = (value * kept).astype(BF16)


def call(kernel, out_shape, args, specs, scratch=(), flops=1000000):
    return pl.pallas_call(
        kernel,
        out_shape=out_shape,
        in_specs=specs,
        out_specs=jax.tree.map(lambda _: VMEM, out_shape),
        scratch_shapes=list(scratch),
        compiler_params=pltpu.CompilerParams(vmem_limit_bytes=32 * 2**20),
        cost_estimate=pl.CostEstimate(flops=flops, bytes_accessed=1000000, transcendentals=0),
    )(*args)


def body(data, recip, gap, owner, weights, start_row, end_row, recorded):
    src_here = lax.axis_index("src")
    freq_here = lax.axis_index("freq")
    src_count = lax.axis_size("src")
    total_out = weights.shape[3]
    points = data.shape[3]

    mine = jnp.swapaxes(recip[:, 0], 1, 2).reshape(2 * NEAR, RECV)
    slots = jnp.arange(src_count, dtype=jnp.int32)
    send = jnp.where((slots == owner[src_here])[:, None, None], mine[None], jnp.zeros_like(mine)[None])
    arrived = lax.all_to_all(send, "src", 0, 0, tiled=True)

    missing = gap == 1
    mask = jnp.pad((~missing).astype(BF16), ((0, 0), (0, RECV - NEAR)), constant_values=1)
    depth = 768
    pred = pl.pallas_call(
        main_product,
        grid=(points // depth,),
        out_shape=jax.ShapeDtypeStruct((2, total_out, RECV), F32),
        in_specs=[
            pl.BlockSpec((RECV, RECV), lambda k: (0, 0)),
            pl.BlockSpec((2, 1, RECV, depth), lambda k: (0, 0, 0, k)),
            pl.BlockSpec((2, 1, depth, total_out), lambda k: (0, 0, k, 0)),
        ],
        out_specs=pl.BlockSpec((2, total_out, RECV), lambda k: (0, 0, 0)),
        scratch_shapes=[pltpu.VMEM((2, RECV, total_out), F32)],
        compiler_params=pltpu.CompilerParams(vmem_limit_bytes=32 * 2**20),
        cost_estimate=pl.CostEstimate(flops=8 * RECV * points * total_out, bytes_accessed=5000000, transcendentals=0),
    )(mask, data, weights)

    near = weights[:, 0, :NEAR, :]
    near_rows = jnp.concatenate(
        [jnp.concatenate([near[0], -near[1]], axis=0), jnp.concatenate([near[1], near[0]], axis=0)], axis=1
    ).T
    gap_rows = missing.T.astype(BF16)
    gap_rows = jnp.concatenate([gap_rows, gap_rows], axis=0)
    parts = call(
        add_fill,
        jax.ShapeDtypeStruct((src_count, 16, RECV), F32),
        (pred, arrived, gap_rows, near_rows),
        [VMEM] * 4,
    )
    parts = lax.all_to_all(parts, "src", 0, 0, tiled=True)
    copies = call(sum_slots, jax.ShapeDtypeStruct((NF, 16, RECV), F32), (parts,), [VMEM])
    spread = lax.all_to_all(copies, "freq", 0, 0, tiled=True).reshape(NF * 16, RECV)

    begin = freq_here * T_DEV - HALO
    lohi = jnp.stack([start_row[0] - begin, end_row[0] - begin]).astype(jnp.int32)
    row = jnp.arange(GROWS, dtype=jnp.int32) // GROUP - LEAD
    keep = (row >= lohi[0]) & (row < lohi[1])
    rows = lax.dynamic_index_in_dim(jnp.asarray(phase_rows()), freq_here, 0, keepdims=False)
    rows = jnp.where(keep[:, None], rows, jnp.zeros_like(rows))
    target = jnp.pad(recorded.reshape(WROWS, -1), ((0, 16), (0, 0)))
    trace_rows = 8 * (WROWS + 2 * LEAD)
    gram, trace = call(
        trace_and_gram,
        (jax.ShapeDtypeStruct((src_count, 8, RECV), F32), jax.ShapeDtypeStruct((trace_rows, RECV), F32)),
        (lohi, spread, rows, target),
        [SMEM, VMEM, VMEM, VMEM],
        [pltpu.VMEM((8 * GROWS, RECV), F32), pltpu.VMEM((GROWS, GROWS), F32)],
    )
    gram = lax.all_to_all(gram, "src", 0, 0, tiled=True)
    damping = float(WROWS * total_out * RECV)
    primaries, filters = call(
        functools.partial(solve_and_filter, damping),
        (jax.ShapeDtypeStruct(recorded.shape, BF16), jax.ShapeDtypeStruct((SIDE, RECV), F32)),
        (lohi, gram, trace, recorded),
        [SMEM, VMEM, VMEM, VMEM],
        [pltpu.VMEM((SIDE, RECV), F32)],
    )
    taps = filters[: GROUP * LAGS_T, 0].reshape(LAGS_T, GROUP)[::-1, :LAGS_X]
    return primaries, taps.reshape(1, -1)


def solution(mesh):
    placed = (
        P(None, "freq", None, "src"),
        P(None, "freq", None, "src"),
        P(None, "src"),
        P(),
        P(None, "freq", "src", None),
        P("freq"),
        P("freq"),
        P("freq", "src", None),
    )
    return jax.shard_map(
        body,
        mesh=mesh,
        in_specs=placed,
        out_specs=(P("freq", "src", None), P("freq", None)),
        check_vma=False,
    )
```

time: 440 us -> 87.2 us (0.20)
  the two profiles are of different devices: /device:TPU:64 before, /device:TPU:8 now
where the time goes in v1:
time: 87.2 us; the launch traced here: 86.4 us
  starting transfers between devices  25.8 us (30%)
  waiting for transfers between devices  22.6 us (26%)
  blocking collectives  15.1 us (17%)
  Pallas kernels  9.84 us (11%)
  local copies, waits for them, and re-layouts  6.34 us (7%)
  other arithmetic  4.68 us (5%)
  between operations  2.04 us (2%)
    all_to_all x1, blocking collectives, body(): gram = lax.all_to_all(gram, 'src', 0, 0, tiled=True)  15.1 us
    all_to_all x1, starting transfers between devices, body(): lax.all_to_all(copies, 'freq', 0, 0, tiled=True).reshape(NF * 16, RECV)  10.4 us
    all_to_all x1, waiting for transfers between devices, body(): parts = lax.all_to_all(parts, 'src', 0, 0, tiled=True)  10.4 us
    all_to_all x1, starting transfers between devices, body(): arrived = lax.all_to_all(send, 'src', 0, 0, tiled=True)  10.2 us
    pallas_call x4, Pallas kernels, call(): pl.pallas_call(kernel, out_shape=out_shape, in_specs=specs, out_specs=jax...  7.81 us
    all_to_all x1, waiting for transfers between devices, body(): lax.all_to_all(copies, 'freq', 0, 0, tiled=True).reshape(NF * 16, RECV)  7.6 us
    all_to_all x1, starting transfers between devices, body(): parts = lax.all_to_all(parts, 'src', 0, 0, tiled=True)  5.25 us
    all_to_all x1, waiting for transfers between devices, body(): arrived = lax.all_to_all(send, 'src', 0, 0, tiled=True)  4.54 us
  transfers between devices with their start and end apart: 3, of which 3 were waited for; matrix products, arithmetic and copies ran while one was open for 4% of the time, Pallas kernels for 2%

profile of v1, /device:TPU:8, one launch (start us, length us, event | category | flops | bytes accessed | tf_op | source)
XLA Modules:
  0.0 86.4 jit_solution(9212792821881567260)
XLA Ops:
  0.6 1.2 %dynamic_slice.7 = s32[1]{0:T(128)} dynamic-slice(s32[32]{0:T(128)} %param.12, s32[]{:T(128)S(6)} %select_n.26), dynamic_slice_sizes={1} | dynamic-slice | bytes 12 | tf_op jit(solution)/shard_map/dynamic_slice | solution.py:230
  1.9 0.6 iota_compare_fusion
  2.5 1.5 %broadcast_select_fusion = bf16[32,32,128]{2,1,0:T(8,128)(2,1)} fusion(pred[32]{0:T(512)(128)(4,1)S(1)} %iota_compare_fusion, bf16[32,128]{1,0:T(8,128)(2,1)} %bitcast.33), kind=kLoop, calls=%fused_computation | loop fusion | flops 131072 | bytes 270368 | tf_op jit(solution)/shard_map/jit(_where)/select_n | solution.py:230
  4.0 10.2 %all-to-all-start = ((bf16[32,32,128]{2,1,0:T(8,128)(2,1)}), bf16[32,32,128]{2,1,0:T(8,128)(2,1)S(1)}, u32[]{:S(2)}, u32[]{:S(2)}) async-start(bf16[32,32,128]{2,1,0:T(8,128)(2,1)} %broadcast_select_fusion), calls=%async_computation | async-start | bytes 524288 | tf_op jit(solution)/shard_map/all_to_all | solution.py:231
  14.2 0.7 fusion.2
  14.9 0.1 copy.17.mask_ref
  15.1 0.7 slice_bitcast_fusion
  15.8 0.7 fusion.1
  16.5 0.1 copy.18
  16.6 0.0 copy-start
  16.6 1.9 %copy-done = bf16[2,1,3072,256]{3,2,1,0:T(8,128)(2,1)S(1)} copy-done((bf16[2,1,3072,256]{3,2,1,0:T(8,128)(2,1)S(1)}, bf16[2,1,3072,256]{3,2,1,0:T(8,128)(2,1)}, u32[]{:S(2)}) %copy-start) | copy-done | bytes 3145752
  18.5 0.0 copy-start.1
  18.5 1.4 %copy-done.1 = bf16[2,1,128,3072]{3,2,1,0:T(8,128)(2,1)S(1)} copy-done((bf16[2,1,128,3072]{3,2,1,0:T(8,128)(2,1)S(1)}, bf16[2,1,128,3072]{3,2,1,0:T(8,128)(2,1)}, u32[]{:S(2)}) %copy-start.1) | copy-done | bytes 1572888
  19.9 0.0 copy-start.2
  19.9 2.0 %shard_map.104.pred_ref = f32[2,256,128]{2,1,0:T(8,128)S(1)} custom-call(bf16[128,128]{1,0:T(8,128)(2,1)S(1)} %copy.17.mask_ref, bf16[2,1,128,3072]{3,2,1,0:T(8,128)(2,1)S(1)} %copy-done.1, bf16[2,1,3072,256]{3,2,1,0:T(8,128)(2,1)S(1)} %copy-done), custom_call_target="tpu_custom_call" | custom-call | flops 805306368 | bytes 5000000 | tf_op jit(solution)/shard_map/pallas_call | solution.py:236
  22.0 4.5 %all-to-all-done.recip_ref = bf16[32,32,128]{2,1,0:T(8,128)(2,1)S(1)} async-done(((bf16[32,32,128]{2,1,0:T(8,128)(2,1)}), bf16[32,32,128]{2,1,0:T(8,128)(2,1)S(1)}, u32[]{:S(2)}, u32[]{:S(2)}) %all-to-all-start) | async-done | bytes 262176 | tf_op jit(solution)/shard_map/all_to_all | solution.py:231
  26.5 0.9 %shard_map.105 = f32[32,16,128]{2,1,0:T(8,128)} custom-call(f32[2,256,128]{2,1,0:T(8,128)S(1)} %shard_map.104.pred_ref, bf16[32,32,128]{2,1,0:T(8,128)(2,1)S(1)} %all-to-all-done.recip_ref, bf16[32,128]{1,0:T(8,128)(2,1)S(1)} %add_convert_fusion.gap_ref, bf16[512,32]{1,0:T(8,128)(2,1)S(1)} %bitcast.28), custom_call_target="tpu_custom_call" | custom-call | flops 1000000 | bytes 1000000 | tf_op jit(solution)/shard_map/pallas_call | solution.py:210
  27.4 5.3 %all-to-all-start.1 = ((f32[32,16,128]{2,1,0:T(8,128)}), f32[32,16,128]{2,1,0:T(8,128)S(1)}, u32[]{:S(2)}, u32[]{:S(2)}) async-start(f32[32,16,128]{2,1,0:T(8,128)} %shard_map.105), calls=%async_computation.1 | async-start | bytes 524288 | tf_op jit(solution)/shard_map/all_to_all | solution.py:263
  34.0 10.4 %all-to-all-done.1.part_ref = f32[32,16,128]{2,1,0:T(8,128)S(1)} async-done(((f32[32,16,128]{2,1,0:T(8,128)}), f32[32,16,128]{2,1,0:T(8,128)S(1)}, u32[]{:S(2)}, u32[]{:S(2)}) %all-to-all-start.1) | async-done | bytes 262176 | tf_op jit(solution)/shard_map/all_to_all | solution.py:263
  44.4 0.7 shard_map.106
  45.1 10.4 %all-to-all-start.2 = ((f32[16,16,128]{2,1,0:T(8,128)}), f32[16,16,128]{2,1,0:T(8,128)S(1)}, u32[]{:S(2)}, u32[]{:S(2)}) async-start(f32[16,16,128]{2,1,0:T(8,128)} %shard_map.106), calls=%async_computation.2 | async-start | bytes 262144 | tf_op jit(solution)/shard_map/all_to_all | solution.py:265
  55.5 0.1 pad_add_fusion.lohi_ref
  55.6 0.0 copy-done.2
  55.7 1.0 %bitcast_select_fusion.rows_ref = bf16[256,256]{1,0:T(8,128)(2,1)S(1)} fusion(bf16[16,256,256]{2,1,0:T(8,128)(2,1)} %constant.52.clone, s32[]{:T(128)S(6)} %select_n.29, pred[256]{0:T(512)(128)(4,1)S(1)} %compare_and_fusion), kind=kLoop, calls=%fused_computation.1 | loop fusion | flops 65536 | bytes 262404 | tf_op jit(solution)/shard_map/jit(_where)/select_n | solution.py:272
  56.7 7.6 %all-to-all-done.2 = f32[16,16,128]{2,1,0:T(8,128)S(1)} async-done(((f32[16,16,128]{2,1,0:T(8,128)}), f32[16,16,128]{2,1,0:T(8,128)S(1)}, u32[]{:S(2)}, u32[]{:S(2)}) %all-to-all-start.2) | async-done | bytes 131104 | tf_op jit(solution)/shard_map/all_to_all | solution.py:265
  64.3 2.1 %shard_map.107 = (f32[32,8,128]{2,1,0:T(8,128)S(1)}, f32[448,128]{1,0:T(8,128)S(1)}) custom-call(s32[2]{0:T(128)S(1)} %pad_add_fusion.lohi_ref, f32[256,128]{1,0:T(8,128)S(1)} %bitcast.29, bf16[256,256]{1,0:T(8,128)(2,1)S(1)} %bitcast_select_fusion.rows_ref, bf16[64,1024]{1,0:T(8,128)(2,1)S(1)} %pad.12.target_ref), custom_call_target="tpu_custom_call" | custom-call | flops 1000000 | bytes 1000000 | tf_op jit(solution)/shard_map/pallas_call | solution.py:210
  66.4 15.1 %all_to_all.20.gram_ref = f32[32,8,128]{2,1,0:T(8,128)S(1)} all-to-all(f32[32,8,128]{2,1,0:T(8,128)S(1)} %get-tuple-element.6), channel_id=1, replica_groups=mesh['freq'=16,'src'=32] {'src'}, dimensions={0} | all-to-all | bytes 262144 | tf_op jit(solution)/shard_map/all_to_all | solution.py:282
  81.5 4.1 %shard_map.108 = (bf16[48,8,128]{2,1,0:T(8,128)(2,1)}, f32[40,128]{1,0:T(8,128)S(1)}) custom-call(s32[2]{0:T(128)S(1)} %pad_add_fusion.lohi_ref, f32[32,8,128]{2,1,0:T(8,128)S(1)} %all_to_all.20.gram_ref, f32[448,128]{1,0:T(8,128)S(1)} %get-tuple-element.7.trace_ref, bf16[48,8,128]{2,1,0:T(8,128)(2,1)S(1)} %copy-done.2), custom_call_target="tpu_custom_call" | custom-call | flops 1000000 | bytes 1000000 | tf_op jit(solution)/shard_map/pallas_call | solution.py:210
  85.6 0.1 slice_reduce_fusion
  85.7 0.1 reshape_squeeze.3
  85.8 0.6 reshape.41
  (7 shorter events, 0.1 us)
Async XLA Ops:
  4.0 22.5 %all-to-all-start = ((bf16[32,32,128]{2,1,0:T(8,128)(2,1)}), bf16[32,32,128]{2,1,0:T(8,128)(2,1)S(1)}, u32[]{:S(2)}, u32[]{:S(2)}) async-start(bf16[32,32,128]{2,1,0:T(8,128)(2,1)} %broadcast_select_fusion), calls=%async_computation | async-start | bytes 524288 | tf_op jit(solution)/shard_map/all_to_all | solution.py:231
  16.6 1.9 %copy-start = (bf16[2,1,3072,256]{3,2,1,0:T(8,128)(2,1)S(1)}, bf16[2,1,3072,256]{3,2,1,0:T(8,128)(2,1)}, u32[]{:S(2)}) copy-start(bf16[2,1,3072,256]{3,2,1,0:T(8,128)(2,1)} %weights_ref.1) | copy-start | bytes 9437188
  18.5 1.4 %copy-start.1 = (bf16[2,1,128,3072]{3,2,1,0:T(8,128)(2,1)S(1)}, bf16[2,1,128,3072]{3,2,1,0:T(8,128)(2,1)}, u32[]{:S(2)}) copy-start(bf16[2,1,128,3072]{3,2,1,0:T(8,128)(2,1)} %data_ref.1) | copy-start | bytes 4718596
  19.9 35.7 %copy-start.2 = (bf16[48,8,128]{2,1,0:T(8,128)(2,1)S(1)}, bf16[48,8,128]{2,1,0:T(8,128)(2,1)}, u32[]{:S(2)}) copy-start(bf16[48,8,128]{2,1,0:T(8,128)(2,1)} %recorded_ref.1) | copy-start | bytes 294916
  27.4 17.0 %all-to-all-start.1 = ((f32[32,16,128]{2,1,0:T(8,128)}), f32[32,16,128]{2,1,0:T(8,128)S(1)}, u32[]{:S(2)}, u32[]{:S(2)}) async-start(f32[32,16,128]{2,1,0:T(8,128)} %shard_map.105), calls=%async_computation.1 | async-start | bytes 524288 | tf_op jit(solution)/shard_map/all_to_all | solution.py:263
  45.1 19.2 %all-to-all-start.2 = ((f32[16,16,128]{2,1,0:T(8,128)}), f32[16,16,128]{2,1,0:T(8,128)S(1)}, u32[]{:S(2)}, u32[]{:S(2)}) async-start(f32[16,16,128]{2,1,0:T(8,128)} %shard_map.106), calls=%async_computation.2 | async-start | bytes 262144 | tf_op jit(solution)/shard_map/all_to_all | solution.py:265

commit v2 on v1

--- a/solution.py
+++ b/solution.py
@@ -24,9 +24,11 @@
 GROUP = 4
 GROWS = 256
 SIDE = 40
+UNKNOWNS = LAGS_T * LAGS_X
 TARGET_COL = GROUP * LEAD + 3
 CENTRE_ROW = GROUP * LEAD + 1
 PACK_AT = (0, 40, 72, 96, 112)
+LOW_AT, RECIP_AT, GAP_AT, NEAR_AT, SLOT_ROWS = 16, 32, 64, 80, 96
 VMEM = pl.BlockSpec(memory_space=pltpu.VMEM)
 SMEM = pl.BlockSpec(memory_space=pltpu.SMEM)
 F32 = jnp.float32
@@ -61,16 +63,37 @@
     return table
 
 
-def main_product(mask_ref, data_ref, weights_ref, out_ref, acc_ref):
+def main_product(gap_ref, recip_ref, data_ref, weights_ref, out_ref, acc_ref, mask_ref):
     step = pl.program_id(0)
     depth = data_ref.shape[3]
+    slots = out_ref.shape[0]
 
     @pl.when(step == 0)
     def _():
         acc_ref[...] = jnp.zeros_like(acc_ref)
+        gap = jnp.where(gap_ref[...] == 1, 1.0, 0.0)
+        full = jnp.concatenate([gap, jnp.zeros((RECV - NEAR, RECV), F32)], axis=0)
+        mask_ref[...] = (1.0 - full.T).astype(BF16)
+        out_ref[:, RECIP_AT:GAP_AT] = jnp.broadcast_to(recip_ref[...][None], (slots, 2 * NEAR, RECV))
+        out_ref[:, GAP_AT:NEAR_AT] = jnp.broadcast_to(gap.astype(BF16)[None], (slots, NEAR, RECV))
+        lanes = lax.broadcasted_iota(jnp.int32, (NEAR, RECV), 1)
+        for group in range(slots * 8 // 64):
+            at = RECV * (group // 2)
+            real = weights_ref[0, 0, :NEAR, at : at + RECV].astype(F32)
+            imag = weights_ref[1, 0, :NEAR, at : at + RECV].astype(F32)
+            if group % 2:
+                real = pltpu.roll(real, 64, 1)
+            else:
+                imag = pltpu.roll(imag, 64, 1)
+            near = jnp.where(lanes < 64, real, imag).astype(BF16)
+            out_ref[8 * group : 8 * group + 8, NEAR_AT:] = jnp.broadcast_to(near[None], (8, NEAR, RECV))
+
+    @pl.when(step == 1)
+    def _():
+        mask_ref[...] = jnp.ones_like(mask_ref)
 
     panel = data_ref[...].reshape(2 * RECV, depth)
-    mask = jnp.where(step == 0, mask_ref[...], jnp.ones_like(mask_ref))
+    mask = mask_ref[...]
     near = panel[:, :RECV] * jnp.concatenate([mask, mask], axis=0)
     panel = jnp.concatenate([near, panel[:, RECV:]], axis=1)
     both = jnp.concatenate([weights_ref[0, 0], weights_ref[1, 0]], axis=1)
@@ -81,23 +104,34 @@
 
     @pl.when(step == pl.num_programs(0) - 1)
     def _():
-        out_ref[0] = acc_ref[0].T
-        out_ref[1] = acc_ref[1].T
-
-
-def add_fill(pred_ref, recip_ref, gap_ref, near_ref, out_ref):
-    slots = out_ref.shape[0]
-    piece = jnp.sum(recip_ref[...].astype(F32), axis=0).astype(BF16)
-    fill = jnp.dot(near_ref[...], piece * gap_ref[...], preferred_element_type=F32)
-    total = pred_ref[...].reshape(fill.shape) + fill
-    half = slots * 8
-    out_ref[:, :8, :] = total[:half].reshape(slots, 8, RECV)
-    out_ref[:, 8:, :] = total[half:].reshape(slots, 8, RECV)
-
-
-def sum_slots(part_ref, out_ref):
-    total = jnp.sum(part_ref[...], axis=0)
-    out_ref[...] = jnp.broadcast_to(total[None], out_ref.shape)
+        real = acc_ref[0].T.reshape(slots, 8, RECV)
+        imag = acc_ref[1].T.reshape(slots, 8, RECV)
+        high, low = two_parts(jnp.concatenate([real, imag], axis=1))
+        out_ref[:, :LOW_AT] = high
+        out_ref[:, LOW_AT:RECIP_AT] = low
+
+
+def sum_and_fill(owner_ref, place_ref, part_ref, out_ref, z_ref, w_ref, f_ref):
+    slots = part_ref.shape[0]
+    total = jnp.zeros((16, RECV), F32)
+    for j in range(slots):
+        total = total + part_ref[j, :LOW_AT].astype(F32) + part_ref[j, LOW_AT:RECIP_AT].astype(F32)
+        block = owner_ref[j]
+        gap = part_ref[block, GAP_AT:NEAR_AT]
+        at = slice(NEAR * j, NEAR * j + NEAR)
+        z_ref[at, :RECV] = part_ref[j, RECIP_AT : RECIP_AT + NEAR] * gap
+        z_ref[at, RECV:] = part_ref[j, RECIP_AT + NEAR : GAP_AT] * gap
+        w_ref[at, :] = part_ref[block, NEAR_AT:]
+    f_ref[...] = lax.dot_general(
+        w_ref[...], z_ref[...], (((0,), (0,)), ((), ())), preferred_element_type=F32
+    )
+    at = pl.multiple_of(place_ref[0] * 8, 8)
+    by_real = f_ref[pl.ds(at, 8), :]
+    by_imag = f_ref[pl.ds(at + 64, 8), :]
+    real = total[:8] + by_real[:, :RECV] - by_imag[:, RECV:]
+    imag = total[8:] + by_imag[:, :RECV] + by_real[:, RECV:]
+    out_ref[:, :8] = jnp.broadcast_to(real[None], (out_ref.shape[0], 8, RECV))
+    out_ref[:, 8:] = jnp.broadcast_to(imag[None], (out_ref.shape[0], 8, RECV))
 
 
 def two_parts(x):
@@ -187,8 +221,9 @@
         column = jnp.broadcast_to(system[:, k : k + 1], (SIDE, RECV))
         scaled = pivot_row / jnp.broadcast_to(system[k : k + 1, k : k + 1], (1, RECV))
         system = jnp.where(row == k, scaled, system - column * scaled)
+    chosen = (lane < UNKNOWNS) & (row == GROUP * (LAGS_T - 1 - lane // LAGS_X) + lane % LAGS_X)
     h_ref[...] = jnp.broadcast_to(system[:, TARGET_COL : TARGET_COL + 1], (SIDE, RECV))
-    filters_ref[...] = h_ref[...]
+    filters_ref[...] = jnp.sum(jnp.where(chosen, h_ref[...], 0.0), axis=0, keepdims=True)[:, :UNKNOWNS]
     first, last = lohi_ref[0], lohi_ref[1]
     recv = lax.broadcasted_iota(jnp.int32, (8, RECV), 1)
     taps = [[jnp.broadcast_to(h_ref[GROUP * p + c : GROUP * p + c + 1, :], (8, RECV)) for c in range(LAGS_X)] for p in range(LAGS_T)]
@@ -225,43 +260,35 @@
     total_out = weights.shape[3]
     points = data.shape[3]
 
-    mine = jnp.swapaxes(recip[:, 0], 1, 2).reshape(2 * NEAR, RECV)
-    slots = jnp.arange(src_count, dtype=jnp.int32)
-    send = jnp.where((slots == owner[src_here])[:, None, None], mine[None], jnp.zeros_like(mine)[None])
-    arrived = lax.all_to_all(send, "src", 0, 0, tiled=True)
-
-    missing = gap == 1
-    mask = jnp.pad((~missing).astype(BF16), ((0, 0), (0, RECV - NEAR)), constant_values=1)
+    recip_rows = jnp.swapaxes(recip[:, 0], 1, 2).reshape(2 * NEAR, RECV)
     depth = 768
-    pred = pl.pallas_call(
+    parts = pl.pallas_call(
         main_product,
         grid=(points // depth,),
-        out_shape=jax.ShapeDtypeStruct((2, total_out, RECV), F32),
+        out_shape=jax.ShapeDtypeStruct((src_count, SLOT_ROWS, RECV), BF16),
         in_specs=[
-            pl.BlockSpec((RECV, RECV), lambda k: (0, 0)),
+            pl.BlockSpec((NEAR, RECV), lambda k: (0, 0)),
+            pl.BlockSpec((2 * NEAR, RECV), lambda k: (0, 0)),
             pl.BlockSpec((2, 1, RECV, depth), lambda k: (0, 0, 0, k)),
             pl.BlockSpec((2, 1, depth, total_out), lambda k: (0, 0, k, 0)),
         ],
-        out_specs=pl.BlockSpec((2, total_out, RECV), lambda k: (0, 0, 0)),
-        scratch_shapes=[pltpu.VMEM((2, RECV, total_out), F32)],
-        compiler_params=pltpu.CompilerParams(vmem_limit_bytes=32 * 2**20),
+        out_specs=pl.BlockSpec((src_count, SLOT_ROWS, RECV), lambda k: (0, 0, 0)),
+        scratch_shapes=[pltpu.VMEM((2, RECV, total_out), F32), pltpu.VMEM((RECV, RECV), BF16)],
         cost_estimate=pl.CostEstimate(flops=8 * RECV * points * total_out, bytes_accessed=5000000, transcendentals=0),
-    )(mask, data, weights)
-
-    near = weights[:, 0, :NEAR, :]
-    near_rows = jnp.concatenate(
-        [jnp.concatenate([near[0], -near[1]], axis=0), jnp.concatenate([near[1], near[0]], axis=0)], axis=1
-    ).T
-    gap_rows = missing.T.astype(BF16)
-    gap_rows = jnp.concatenate([gap_rows, gap_rows], axis=0)
-    parts = call(
-        add_fill,
-        jax.ShapeDtypeStruct((src_count, 16, RECV), F32),
-        (pred, arrived, gap_rows, near_rows),
-        [VMEM] * 4,
-    )
+    )(gap.T, recip_rows, data, weights)
     parts = lax.all_to_all(parts, "src", 0, 0, tiled=True)
-    copies = call(sum_slots, jax.ShapeDtypeStruct((NF, 16, RECV), F32), (parts,), [VMEM])
+    place = jnp.reshape(src_here % 8, (1,)).astype(jnp.int32)
+    copies = call(
+        sum_and_fill,
+        jax.ShapeDtypeStruct((NF, 16, RECV), F32),
+        (owner, place, parts),
+        [SMEM, SMEM, VMEM],
+        [
+            pltpu.VMEM((NEAR * src_count, 2 * RECV), BF16),
+            pltpu.VMEM((NEAR * src_count, RECV), BF16),
+            pltpu.VMEM((RECV, 2 * RECV), F32),
+        ],
+    )
     spread = lax.all_to_all(copies, "freq", 0, 0, tiled=True).reshape(NF * 16, RECV)
 
     begin = freq_here * T_DEV - HALO
@@ -283,13 +310,12 @@
     damping = float(WROWS * total_out * RECV)
     primaries, filters = call(
         functools.partial(solve_and_filter, damping),
-        (jax.ShapeDtypeStruct(recorded.shape, BF16), jax.ShapeDtypeStruct((SIDE, RECV), F32)),
+        (jax.ShapeDtypeStruct(recorded.shape, BF16), jax.ShapeDtypeStruct((1, UNKNOWNS), F32)),
         (lohi, gram, trace, recorded),
         [SMEM, VMEM, VMEM, VMEM],
         [pltpu.VMEM((SIDE, RECV), F32)],
     )
-    taps = filters[: GROUP * LAGS_T, 0].reshape(LAGS_T, GROUP)[::-1, :LAGS_X]
-    return primaries, taps.reshape(1, -1)
+    return primaries, filters
 
 
 def solution(mesh):

time: 87.2 us -> 81.8 us (0.938)
  waiting for transfers between devices: 22.6 us -> 29.4 us
  local copies, waits for them, and re-layouts: 6.34 us -> 0.03 us
  starting transfers between devices: 25.8 us -> 20.7 us
  other arithmetic: 4.68 us -> 1.1 us
  Pallas kernels: 9.84 us -> 12.6 us
    all_to_all x1, waiting for transfers between devices: 10.4 us -> 21.8 us  [body(): parts = lax.all_to_all(parts, 'src', 0, 0, tiled=True)]
    all_to_all x1 -> x0, starting transfers between devices: 10.2 us -> none  [body(): arrived = lax.all_to_all(send, 'src', 0, 0, tiled=True)]
    all_to_all x1, starting transfers between devices: 5.25 us -> 10.3 us  [body(): parts = lax.all_to_all(parts, 'src', 0, 0, tiled=True)]
    all_to_all x1 -> x0, waiting for transfers between devices: 4.54 us -> none  [body(): arrived = lax.all_to_all(send, 'src', 0, 0, tiled=True)]
    unnamed x7 -> x5, local copies, waits for them, and re-layouts: 3.31 us -> 0.02 us
    pallas_call x1, Pallas kernels: 2.03 us -> 4.95 us  [body(): pl.pallas_call(main_product, grid=(points // depth,), out_shape=jax.Shape...]
    select_n x1 -> x0, other arithmetic: 1.52 us -> none  [body(): jnp.where((slots == owner[src_here])[:, None, None], mine[None], jnp.zero...]
    dynamic_slice x1 -> x0, local copies, waits for them, and re-layouts: 1.24 us -> none  [body(): owner[src_here]]
  transfers between devices with their start and end apart: 3 -> 2, of which waited for: 3 -> 2; matrix products, arithmetic and copies ran while one was open for 4% -> 1% of each run, Pallas kernels for 2% -> 0%
where the time goes in v2:
time: 81.8 us; the launch traced here: 81.4 us
  waiting for transfers between devices  29.4 us (36%)
  starting transfers between devices  20.7 us (25%)
  blocking collectives  15.4 us (19%)
  Pallas kernels  12.6 us (15%)
  between operations  2 us (2%)
  other arithmetic  1.1 us (1%)
    all_to_all x1, waiting for transfers between devices, body(): parts = lax.all_to_all(parts, 'src', 0, 0, tiled=True)  21.8 us
    all_to_all x1, blocking collectives, body(): gram = lax.all_to_all(gram, 'src', 0, 0, tiled=True)  15.4 us
    all_to_all x1, starting transfers between devices, body(): lax.all_to_all(copies, 'freq', 0, 0, tiled=True).reshape(NF * 16, RECV)  10.4 us
    all_to_all x1, starting transfers between devices, body(): parts = lax.all_to_all(parts, 'src', 0, 0, tiled=True)  10.3 us
    pallas_call x3, Pallas kernels, call(): pl.pallas_call(kernel, out_shape=out_shape, in_specs=specs, out_specs=jax...  7.7 us
    all_to_all x1, waiting for transfers between devices, body(): lax.all_to_all(copies, 'freq', 0, 0, tiled=True).reshape(NF * 16, RECV)  7.6 us
    pallas_call x1, Pallas kernels, body(): pl.pallas_call(main_product, grid=(points // depth,), out_shape=jax.Shape...  4.95 us
  transfers between devices with their start and end apart: 2, of which 2 were waited for; matrix products, arithmetic and copies ran while one was open for 1% of the time, Pallas kernels for 0%

profile of v2, /device:TPU:8, one launch (start us, length us, event | category | flops | bytes accessed | tf_op | source)
XLA Modules:
  0.0 81.4 jit_solution(15517980652805796675)
XLA Ops:
  0.6 0.0 copy-start.1
  0.6 4.9 %shard_map.104 = bf16[32,96,128]{2,1,0:T(8,128)(2,1)} custom-call(s32[16,128]{1,0:T(8,128)} %bitcast.23, bf16[32,128]{1,0:T(8,128)(2,1)} %bitcast.24, bf16[2,1,128,3072]{3,2,1,0:T(8,128)(2,1)} %data_ref.1, bf16[2,1,3072,256]{3,2,1,0:T(8,128)(2,1)} %weights_ref.1), custom_call_target="tpu_custom_call" | custom-call | flops 805306368 | bytes 5000000 | tf_op jit(solution)/shard_map/pallas_call | solution.py:265
  5.6 0.0 copy-start
  5.6 10.3 %all-to-all-start = ((bf16[32,96,128]{2,1,0:T(8,128)(2,1)}), bf16[32,96,128]{2,1,0:T(8,128)(2,1)S(1)}, u32[]{:S(2)}, u32[]{:S(2)}) async-start(bf16[32,96,128]{2,1,0:T(8,128)(2,1)} %shard_map.104), calls=%async_computation | async-start | bytes 1572864 | tf_op jit(solution)/shard_map/all_to_all | solution.py:279
  17.2 21.8 %all-to-all-done.part_ref = bf16[32,96,128]{2,1,0:T(8,128)(2,1)S(1)} async-done(((bf16[32,96,128]{2,1,0:T(8,128)(2,1)}), bf16[32,96,128]{2,1,0:T(8,128)(2,1)S(1)}, u32[]{:S(2)}, u32[]{:S(2)}) %all-to-all-start) | async-done | bytes 786464 | tf_op jit(solution)/shard_map/all_to_all | solution.py:279
  39.1 0.0 copy-done.1
  39.1 1.5 %shard_map.105 = f32[16,16,128]{2,1,0:T(8,128)} custom-call(s32[32]{0:T(128)S(1)} %copy-done.1, s32[1]{0:T(128)} %bitcast.4.place_ref, bf16[32,96,128]{2,1,0:T(8,128)(2,1)S(1)} %all-to-all-done.part_ref), custom_call_target="tpu_custom_call" | custom-call | flops 1000000 | bytes 1000000 | tf_op jit(solution)/shard_map/pallas_call | solution.py:245
  40.5 10.4 %all-to-all-start.1 = ((f32[16,16,128]{2,1,0:T(8,128)}), f32[16,16,128]{2,1,0:T(8,128)S(1)}, u32[]{:S(2)}, u32[]{:S(2)}) async-start(f32[16,16,128]{2,1,0:T(8,128)} %shard_map.105), calls=%async_computation.1 | async-start | bytes 262144 | tf_op jit(solution)/shard_map/all_to_all | solution.py:292
  51.0 0.1 pad_add_fusion.lohi_ref
  51.1 0.0 copy-done
  51.1 1.0 %bitcast_select_fusion.rows_ref = bf16[256,256]{1,0:T(8,128)(2,1)S(1)} fusion(bf16[16,256,256]{2,1,0:T(8,128)(2,1)} %constant.57.clone, s32[]{:T(128)S(6)} %select_n.28, pred[256]{0:T(512)(128)(4,1)S(1)} %compare_and_fusion), kind=kLoop, calls=%fused_computation | loop fusion | flops 65536 | bytes 262404 | tf_op jit(solution)/shard_map/jit(_where)/select_n | solution.py:299
  52.1 7.6 %all-to-all-done.1 = f32[16,16,128]{2,1,0:T(8,128)S(1)} async-done(((f32[16,16,128]{2,1,0:T(8,128)}), f32[16,16,128]{2,1,0:T(8,128)S(1)}, u32[]{:S(2)}, u32[]{:S(2)}) %all-to-all-start.1) | async-done | bytes 131104 | tf_op jit(solution)/shard_map/all_to_all | solution.py:292
  59.7 2.1 %shard_map.106 = (f32[32,8,128]{2,1,0:T(8,128)S(1)}, f32[448,128]{1,0:T(8,128)S(1)}) custom-call(s32[2]{0:T(128)S(1)} %pad_add_fusion.lohi_ref, f32[256,128]{1,0:T(8,128)S(1)} %bitcast.20, bf16[256,256]{1,0:T(8,128)(2,1)S(1)} %bitcast_select_fusion.rows_ref, bf16[64,1024]{1,0:T(8,128)(2,1)S(1)} %pad.4.target_ref), custom_call_target="tpu_custom_call" | custom-call | flops 1000000 | bytes 1000000 | tf_op jit(solution)/shard_map/pallas_call | solution.py:245
  61.9 15.4 %all_to_all.15.gram_ref = f32[32,8,128]{2,1,0:T(8,128)S(1)} all-to-all(f32[32,8,128]{2,1,0:T(8,128)S(1)} %get-tuple-element.4), channel_id=1, replica_groups=mesh['freq'=16,'src'=32] {'src'}, dimensions={0} | all-to-all | bytes 262144 | tf_op jit(solution)/shard_map/all_to_all | solution.py:309
  77.3 4.1 %shard_map.107 = (bf16[48,8,128]{2,1,0:T(8,128)(2,1)}, f32[1,27]{1,0:T(1,128)}) custom-call(s32[2]{0:T(128)S(1)} %pad_add_fusion.lohi_ref, f32[32,8,128]{2,1,0:T(8,128)S(1)} %all_to_all.15.gram_ref, f32[448,128]{1,0:T(8,128)S(1)} %get-tuple-element.5.trace_ref, bf16[48,8,128]{2,1,0:T(8,128)(2,1)S(1)} %copy-done), custom_call_target="tpu_custom_call" | custom-call | flops 1000000 | bytes 1000000 | tf_op jit(solution)/shard_map/pallas_call | solution.py:245
  (3 shorter events, 0.0 us)
Async XLA Ops:
  0.6 38.4 %copy-start.1 = (s32[32]{0:T(128)S(1)}, s32[32]{0:T(128)}, u32[]{:S(2)}) copy-start(s32[32]{0:T(128)} %owner_ref.1) | copy-start | bytes 388
  5.6 45.5 %copy-start = (bf16[48,8,128]{2,1,0:T(8,128)(2,1)S(1)}, bf16[48,8,128]{2,1,0:T(8,128)(2,1)}, u32[]{:S(2)}) copy-start(bf16[48,8,128]{2,1,0:T(8,128)(2,1)} %recorded_ref.1) | copy-start | bytes 294916
  5.6 33.5 %all-to-all-start = ((bf16[32,96,128]{2,1,0:T(8,128)(2,1)}), bf16[32,96,128]{2,1,0:T(8,128)(2,1)S(1)}, u32[]{:S(2)}, u32[]{:S(2)}) async-start(bf16[32,96,128]{2,1,0:T(8,128)(2,1)} %shard_map.104), calls=%async_computation | async-start | bytes 1572864 | tf_op jit(solution)/shard_map/all_to_all | solution.py:279
  40.5 19.2 %all-to-all-start.1 = ((f32[16,16,128]{2,1,0:T(8,128)}), f32[16,16,128]{2,1,0:T(8,128)S(1)}, u32[]{:S(2)}, u32[]{:S(2)}) async-start(f32[16,16,128]{2,1,0:T(8,128)} %shard_map.105), calls=%async_computation.1 | async-start | bytes 262144 | tf_op jit(solution)/shard_map/all_to_all | solution.py:292

commit v3 on v2

--- a/solution.py
+++ b/solution.py
@@ -30,7 +30,6 @@
 PACK_AT = (0, 40, 72, 96, 112)
 LOW_AT, RECIP_AT, GAP_AT, NEAR_AT, SLOT_ROWS = 16, 32, 64, 80, 96
 VMEM = pl.BlockSpec(memory_space=pltpu.VMEM)
-SMEM = pl.BlockSpec(memory_space=pltpu.SMEM)
 F32 = jnp.float32
 BF16 = jnp.bfloat16
 
@@ -111,12 +110,17 @@
         out_ref[:, LOW_AT:RECIP_AT] = low
 
 
-def sum_and_fill(owner_ref, place_ref, part_ref, out_ref, z_ref, w_ref, f_ref):
+def sum_and_fill(owner_ref, part_ref, out_ref, z_ref, w_ref, f_ref, block_ref, sem):
     slots = part_ref.shape[0]
+    copy = pltpu.make_async_copy(owner_ref, block_ref, sem)
+    copy.start()
+    place = lax.rem(lax.axis_index("src"), 8)
     total = jnp.zeros((16, RECV), F32)
     for j in range(slots):
         total = total + part_ref[j, :LOW_AT].astype(F32) + part_ref[j, LOW_AT:RECIP_AT].astype(F32)
-        block = owner_ref[j]
+    copy.wait()
+    for j in range(slots):
+        block = block_ref[j]
         gap = part_ref[block, GAP_AT:NEAR_AT]
         at = slice(NEAR * j, NEAR * j + NEAR)
         z_ref[at, :RECV] = part_ref[j, RECIP_AT : RECIP_AT + NEAR] * gap
@@ -125,7 +129,7 @@
     f_ref[...] = lax.dot_general(
         w_ref[...], z_ref[...], (((0,), (0,)), ((), ())), preferred_element_type=F32
     )
-    at = pl.multiple_of(place_ref[0] * 8, 8)
+    at = pl.multiple_of(place * 8, 8)
     by_real = f_ref[pl.ds(at, 8), :]
     by_imag = f_ref[pl.ds(at + 64, 8), :]
     real = total[:8] + by_real[:, :RECV] - by_imag[:, RECV:]
@@ -139,7 +143,7 @@
     return high, (x - high.astype(F32)).astype(BF16)
 
 
-def trace_and_gram(lohi_ref, x_ref, rows_ref, target_ref, gram_ref, trace_ref, a_ref, g_ref):
+def trace_and_gram(keep_ref, x_ref, rows_ref, target_ref, gram_ref, trace_ref, a_ref, g_ref):
     sources = 8
     x = jnp.concatenate([x_ref[pl.ds(s, 2 * NF, stride=sources), :] for s in range(sources)], axis=1)
     high, rest = x.astype(BF16), x
@@ -174,7 +178,6 @@
     g_ref[...] = lax.dot_general(high, high, dims, preferred_element_type=F32) + 2.0 * lax.dot_general(
         high, low, dims, preferred_element_type=F32
     )
-    first, last = lohi_ref[0], lohi_ref[1]
     total = jnp.zeros((SIDE, RECV), F32)
     for u in range(WROWS):
         at = GROUP * u
@@ -186,8 +189,7 @@
             part = pltpu.roll(part, (2 * RECV - at) % RECV, 1)
         else:
             part = pltpu.roll(g_ref[at : at + SIDE, :], 2 * RECV - at, 1)[:, :RECV]
-        kept = jnp.where((u >= first) & (u < last), 1.0, 0.0)
-        total = total + part * kept
+        total = total + part * keep_ref[u : u + 1, :]
     full = jnp.concatenate([total, jnp.zeros((RECV - SIDE, RECV), F32)], axis=0)
     total = 0.5 * (total + full.T[:SIDE])
     lanes = lax.broadcasted_iota(jnp.int32, (8, RECV), 1)
@@ -199,7 +201,7 @@
     gram_ref[...] = jnp.broadcast_to(packed[None], gram_ref.shape)
 
 
-def solve_and_filter(damping, lohi_ref, gram_ref, trace_ref, recorded_ref, out_ref, filters_ref, h_ref):
+def solve_and_filter(damping, keep_ref, gram_ref, trace_ref, recorded_ref, out_ref, filters_ref, h_ref):
     packed = jnp.sum(gram_ref[...], axis=0)
     lanes = lax.broadcasted_iota(jnp.int32, (8, RECV), 1)
     pieces = []
@@ -214,17 +216,23 @@
     unknown = lax.rem(row, GROUP) < LAGS_X
     system = system + jnp.where((row == lane) & unknown, damping, 0.0)
     system = system + jnp.where((row == CENTRE_ROW) & (lane == TARGET_COL), damping, 0.0)
-    for k in range(GROUP * LAGS_T):
-        if k % GROUP >= LAGS_X:
-            continue
-        pivot_row = system[k : k + 1, :]
-        column = jnp.broadcast_to(system[:, k : k + 1], (SIDE, RECV))
-        scaled = pivot_row / jnp.broadcast_to(system[k : k + 1, k : k + 1], (1, RECV))
-        system = jnp.where(row == k, scaled, system - column * scaled)
+    order = [k for k in range(GROUP * LAGS_T) if k % GROUP < LAGS_X]
+    for one, two in zip(order[:-1:2], order[1::2]):
+        first = jnp.broadcast_to(system[:, one : one + 1], (SIDE, RECV))
+        second = jnp.broadcast_to(system[:, two : two + 1], (SIDE, RECV))
+        top, bottom = system[one : one + 1, :], system[two : two + 1, :]
+        a, b, d = first[one : one + 1], second[one : one + 1], second[two : two + 1]
+        scale = 1.0 / (a * d - b * b)
+        top, bottom = (d * top - b * bottom) * scale, (a * bottom - b * top) * scale
+        rest = system - first * top - second * bottom
+        system = jnp.where(row == one, top, jnp.where(row == two, bottom, rest))
+    last = order[-1]
+    column = jnp.broadcast_to(system[:, last : last + 1], (SIDE, RECV))
+    pivot_row = system[last : last + 1, :] / column[last : last + 1]
+    system = jnp.where(row == last, pivot_row, system - column * pivot_row)
     chosen = (lane < UNKNOWNS) & (row == GROUP * (LAGS_T - 1 - lane // LAGS_X) + lane % LAGS_X)
     h_ref[...] = jnp.broadcast_to(system[:, TARGET_COL : TARGET_COL + 1], (SIDE, RECV))
     filters_ref[...] = jnp.sum(jnp.where(chosen, h_ref[...], 0.0), axis=0, keepdims=True)[:, :UNKNOWNS]
-    first, last = lohi_ref[0], lohi_ref[1]
     recv = lax.broadcasted_iota(jnp.int32, (8, RECV), 1)
     taps = [[jnp.broadcast_to(h_ref[GROUP * p + c : GROUP * p + c + 1, :], (8, RECV)) for c in range(LAGS_X)] for p in range(LAGS_T)]
     for u in range(WROWS):
@@ -236,9 +244,8 @@
                 sums[c] = term if sums[c] is None else sums[c] + term
         ahead = jnp.where(recv < RECV - 1, pltpu.roll(sums[0], RECV - 1, 1), 0.0)
         behind = jnp.where(recv > 0, pltpu.roll(sums[2], 1, 1), 0.0)
-        kept = jnp.where((u >= first) & (u < last), 1.0, 0.0)
         value = recorded_ref[u].astype(F32) - (sums[1] + ahead + behind)
-        out_ref[u] = (value * kept).astype(BF16)
+        out_ref[u] = (value * keep_ref[u : u + 1, :]).astype(BF16)
 
 
 def call(kernel, out_shape, args, specs, scratch=(), flops=1000000):
@@ -254,14 +261,13 @@
 
 
 def body(data, recip, gap, owner, weights, start_row, end_row, recorded):
-    src_here = lax.axis_index("src")
     freq_here = lax.axis_index("freq")
     src_count = lax.axis_size("src")
     total_out = weights.shape[3]
     points = data.shape[3]
 
     recip_rows = jnp.swapaxes(recip[:, 0], 1, 2).reshape(2 * NEAR, RECV)
-    depth = 768
+    depth = points // 2
     parts = pl.pallas_call(
         main_product,
         grid=(points // depth,),
@@ -277,24 +283,27 @@
         cost_estimate=pl.CostEstimate(flops=8 * RECV * points * total_out, bytes_accessed=5000000, transcendentals=0),
     )(gap.T, recip_rows, data, weights)
     parts = lax.all_to_all(parts, "src", 0, 0, tiled=True)
-    place = jnp.reshape(src_here % 8, (1,)).astype(jnp.int32)
     copies = call(
         sum_and_fill,
         jax.ShapeDtypeStruct((NF, 16, RECV), F32),
-        (owner, place, parts),
-        [SMEM, SMEM, VMEM],
+        (owner, parts),
+        [pl.BlockSpec(memory_space=pl.ANY), VMEM],
         [
             pltpu.VMEM((NEAR * src_count, 2 * RECV), BF16),
             pltpu.VMEM((NEAR * src_count, RECV), BF16),
             pltpu.VMEM((RECV, 2 * RECV), F32),
+            pltpu.SMEM((src_count,), jnp.int32),
+            pltpu.SemaphoreType.DMA,
         ],
     )
     spread = lax.all_to_all(copies, "freq", 0, 0, tiled=True).reshape(NF * 16, RECV)
 
     begin = freq_here * T_DEV - HALO
-    lohi = jnp.stack([start_row[0] - begin, end_row[0] - begin]).astype(jnp.int32)
+    first, last = start_row[0] - begin, end_row[0] - begin
+    row = lax.broadcasted_iota(jnp.int32, (WROWS, RECV), 0)
+    keep_rows = ((row >= first) & (row < last)).astype(F32)
     row = jnp.arange(GROWS, dtype=jnp.int32) // GROUP - LEAD
-    keep = (row >= lohi[0]) & (row < lohi[1])
+    keep = (row >= first) & (row < last)
     rows = lax.dynamic_index_in_dim(jnp.asarray(phase_rows()), freq_here, 0, keepdims=False)
     rows = jnp.where(keep[:, None], rows, jnp.zeros_like(rows))
     target = jnp.pad(recorded.reshape(WROWS, -1), ((0, 16), (0, 0)))
@@ -302,8 +311,8 @@
     gram, trace = call(
         trace_and_gram,
         (jax.ShapeDtypeStruct((src_count, 8, RECV), F32), jax.ShapeDtypeStruct((trace_rows, RECV), F32)),
-        (lohi, spread, rows, target),
-        [SMEM, VMEM, VMEM, VMEM],
+        (keep_rows, spread, rows, target),
+        [VMEM] * 4,
         [pltpu.VMEM((8 * GROWS, RECV), F32), pltpu.VMEM((GROWS, GROWS), F32)],
     )
     gram = lax.all_to_all(gram, "src", 0, 0, tiled=True)
@@ -311,8 +320,8 @@
     primaries, filters = call(
         functools.partial(solve_and_filter, damping),
         (jax.ShapeDtypeStruct(recorded.shape, BF16), jax.ShapeDtypeStruct((1, UNKNOWNS), F32)),
-        (lohi, gram, trace, recorded),
-        [SMEM, VMEM, VMEM, VMEM],
+        (keep_rows, gram, trace, recorded),
+        [VMEM] * 4,
         [pltpu.VMEM((SIDE, RECV), F32)],
     )
     return primaries, filters

time: 81.8 us -> 78.9 us (0.965)
  Pallas kernels: 12.6 us -> 9.71 us
    pallas_call x3, Pallas kernels: 7.7 us -> 5.68 us  [call(): pl.pallas_call(kernel, out_shape=out_shape, in_specs=specs, out_specs=jax...]
    pallas_call x1, Pallas kernels: 4.95 us -> 4.03 us  [body(): pl.pallas_call(main_product, grid=(points // depth,), out_shape=jax.Shape...]
where the time goes in v3:
time: 78.9 us; the launch traced here: 78.5 us
  waiting for transfers between devices  29.5 us (37%)
  starting transfers between devices  20.7 us (26%)
  blocking collectives  15.4 us (20%)
  Pallas kernels  9.71 us (12%)
  between operations  2.02 us (3%)
  other arithmetic  1.02 us (1%)
    all_to_all x1, waiting for transfers between devices, body(): parts = lax.all_to_all(parts, 'src', 0, 0, tiled=True)  21.9 us
    all_to_all x1, blocking collectives, body(): gram = lax.all_to_all(gram, 'src', 0, 0, tiled=True)  15.4 us
    all_to_all x1, starting transfers between devices, body(): lax.all_to_all(copies, 'freq', 0, 0, tiled=True).reshape(NF * 16, RECV)  10.4 us
    all_to_all x1, starting transfers between devices, body(): parts = lax.all_to_all(parts, 'src', 0, 0, tiled=True)  10.3 us
    all_to_all x1, waiting for transfers between devices, body(): lax.all_to_all(copies, 'freq', 0, 0, tiled=True).reshape(NF * 16, RECV)  7.66 us
    pallas_call x3, Pallas kernels, call(): pl.pallas_call(kernel, out_shape=out_shape, in_specs=specs, out_specs=jax...  5.68 us
    pallas_call x1, Pallas kernels, body(): pl.pallas_call(main_product, grid=(points // depth,), out_shape=jax.Shape...  4.03 us
  transfers between devices with their start and end apart: 2, of which 2 were waited for; matrix products, arithmetic and copies ran while one was open for 1% of the time, Pallas kernels for 0%

profile of v3, /device:TPU:8, one launch (start us, length us, event | category | flops | bytes accessed | tf_op | source)
XLA Modules:
  0.0 78.5 jit_solution(16419146612591526528)
XLA Ops:
  0.6 0.0 copy-start.1
  0.6 4.0 %shard_map.104 = bf16[32,96,128]{2,1,0:T(8,128)(2,1)} custom-call(s32[16,128]{1,0:T(8,128)} %bitcast.20, bf16[32,128]{1,0:T(8,128)(2,1)} %bitcast.21, bf16[2,1,128,3072]{3,2,1,0:T(8,128)(2,1)} %data_ref.1, bf16[2,1,3072,256]{3,2,1,0:T(8,128)(2,1)} %weights_ref.1), custom_call_target="tpu_custom_call" | custom-call | flops 805306368 | bytes 5000000 | tf_op jit(solution)/shard_map/pallas_call | solution.py:271
  4.7 0.0 copy-start
  4.7 10.3 %all-to-all-start = ((bf16[32,96,128]{2,1,0:T(8,128)(2,1)}), bf16[32,96,128]{2,1,0:T(8,128)(2,1)S(1)}, u32[]{:S(2)}, u32[]{:S(2)}) async-start(bf16[32,96,128]{2,1,0:T(8,128)(2,1)} %shard_map.104), calls=%async_computation | async-start | bytes 1572864 | tf_op jit(solution)/shard_map/all_to_all | solution.py:285
  16.3 21.9 %all-to-all-done.part_ref = bf16[32,96,128]{2,1,0:T(8,128)(2,1)S(1)} async-done(((bf16[32,96,128]{2,1,0:T(8,128)(2,1)}), bf16[32,96,128]{2,1,0:T(8,128)(2,1)S(1)}, u32[]{:S(2)}, u32[]{:S(2)}) %all-to-all-start) | async-done | bytes 786464 | tf_op jit(solution)/shard_map/all_to_all | solution.py:285
  38.1 0.0 copy-done.1
  38.1 1.5 %shard_map.105 = f32[16,16,128]{2,1,0:T(8,128)} custom-call(s32[32]{0:T(128)S(1)} %copy-done.1, bf16[32,96,128]{2,1,0:T(8,128)(2,1)S(1)} %all-to-all-done.part_ref), custom_call_target="tpu_custom_call" | custom-call | flops 1000000 | bytes 1000000 | tf_op jit(solution)/shard_map/pallas_call | solution.py:252
  39.7 10.4 %all-to-all-start.1 = ((f32[16,16,128]{2,1,0:T(8,128)}), f32[16,16,128]{2,1,0:T(8,128)S(1)}, u32[]{:S(2)}, u32[]{:S(2)}) async-start(f32[16,16,128]{2,1,0:T(8,128)} %shard_map.105), calls=%async_computation.1 | async-start | bytes 262144 | tf_op jit(solution)/shard_map/all_to_all | solution.py:299
  50.1 0.0 copy-done
  50.2 1.0 %bitcast_select_fusion.rows_ref = bf16[256,256]{1,0:T(8,128)(2,1)S(1)} fusion(bf16[16,256,256]{2,1,0:T(8,128)(2,1)} %constant.43.clone, s32[]{:T(128)S(6)} %select_n.20, pred[256]{0:T(512)(128)(4,1)S(1)} %compare_and_fusion), kind=kLoop, calls=%fused_computation | loop fusion | flops 65536 | bytes 262404 | tf_op jit(solution)/shard_map/jit(_where)/select_n | solution.py:308
  51.2 7.7 %all-to-all-done.1 = f32[16,16,128]{2,1,0:T(8,128)S(1)} async-done(((f32[16,16,128]{2,1,0:T(8,128)}), f32[16,16,128]{2,1,0:T(8,128)S(1)}, u32[]{:S(2)}, u32[]{:S(2)}) %all-to-all-start.1) | async-done | bytes 131104 | tf_op jit(solution)/shard_map/all_to_all | solution.py:299
  58.8 0.1 iota.17.keep_ref
  58.9 1.6 %shard_map.106 = (f32[32,8,128]{2,1,0:T(8,128)S(1)}, f32[448,128]{1,0:T(8,128)S(1)}) custom-call(f32[48,128]{1,0:T(8,128)S(1)} %iota.17.keep_ref, f32[256,128]{1,0:T(8,128)S(1)} %bitcast.17, bf16[256,256]{1,0:T(8,128)(2,1)S(1)} %bitcast_select_fusion.rows_ref, bf16[64,1024]{1,0:T(8,128)(2,1)S(1)} %pad.4.target_ref), custom_call_target="tpu_custom_call" | custom-call | flops 1000000 | bytes 1000000 | tf_op jit(solution)/shard_map/pallas_call | solution.py:252
  60.5 15.4 %all_to_all.15.gram_ref = f32[32,8,128]{2,1,0:T(8,128)S(1)} all-to-all(f32[32,8,128]{2,1,0:T(8,128)S(1)} %get-tuple-element.4), channel_id=1, replica_groups=mesh['freq'=16,'src'=32] {'src'}, dimensions={0} | all-to-all | bytes 262144 | tf_op jit(solution)/shard_map/all_to_all | solution.py:318
  75.9 2.6 %shard_map.107 = (bf16[48,8,128]{2,1,0:T(8,128)(2,1)}, f32[1,27]{1,0:T(1,128)}) custom-call(f32[48,128]{1,0:T(8,128)S(1)} %iota.17.keep_ref, f32[32,8,128]{2,1,0:T(8,128)S(1)} %all_to_all.15.gram_ref, f32[448,128]{1,0:T(8,128)S(1)} %get-tuple-element.5.trace_ref, bf16[48,8,128]{2,1,0:T(8,128)(2,1)S(1)} %copy-done), custom_call_target="tpu_custom_call" | custom-call | flops 1000000 | bytes 1000000 | tf_op jit(solution)/shard_map/pallas_call | solution.py:252
  (4 shorter events, 0.0 us)
Async XLA Ops:
  0.6 37.5 %copy-start.1 = (s32[32]{0:T(128)S(1)}, s32[32]{0:T(128)}, u32[]{:S(2)}) copy-start(s32[32]{0:T(128)} %owner_ref.1) | copy-start | bytes 388
  4.7 45.4 %copy-start = (bf16[48,8,128]{2,1,0:T(8,128)(2,1)S(1)}, bf16[48,8,128]{2,1,0:T(8,128)(2,1)}, u32[]{:S(2)}) copy-start(bf16[48,8,128]{2,1,0:T(8,128)(2,1)} %recorded_ref.1) | copy-start | bytes 294916
  4.7 33.5 %all-to-all-start = ((bf16[32,96,128]{2,1,0:T(8,128)(2,1)}), bf16[32,96,128]{2,1,0:T(8,128)(2,1)S(1)}, u32[]{:S(2)}, u32[]{:S(2)}) async-start(bf16[32,96,128]{2,1,0:T(8,128)(2,1)} %shard_map.104), calls=%async_computation | async-start | bytes 1572864 | tf_op jit(solution)/shard_map/all_to_all | solution.py:285
  39.7 19.2 %all-to-all-start.1 = ((f32[16,16,128]{2,1,0:T(8,128)}), f32[16,16,128]{2,1,0:T(8,128)S(1)}, u32[]{:S(2)}, u32[]{:S(2)}) async-start(f32[16,16,128]{2,1,0:T(8,128)} %shard_map.105), calls=%async_computation.1 | async-start | bytes 262144 | tf_op jit(solution)/shard_map/all_to_all | solution.py:299

commit v4 on v3

--- a/solution.py
+++ b/solution.py
@@ -8,7 +8,7 @@
 from jax import lax
 from jax.experimental import pallas as pl
 from jax.experimental.pallas import tpu as pltpu
-from jax.sharding import PartitionSpec as P
+from jax.sharding import Mesh, PartitionSpec as P
 
 RECV = 128
 NFFT = 512
@@ -28,7 +28,8 @@
 TARGET_COL = GROUP * LEAD + 3
 CENTRE_ROW = GROUP * LEAD + 1
 PACK_AT = (0, 40, 72, 96, 112)
-LOW_AT, RECIP_AT, GAP_AT, NEAR_AT, SLOT_ROWS = 16, 32, 64, 80, 96
+LOW_AT, RECIP_AT, GAP_AT, SLOT_ROWS = 16, 32, 48, 64
+HALF = RECV // 2
 VMEM = pl.BlockSpec(memory_space=pltpu.VMEM)
 F32 = jnp.float32
 BF16 = jnp.bfloat16
@@ -54,7 +55,7 @@
                 continue
             turns = (F_LOW + freqs) * time % NFFT
             angle = turns * (2.0 * math.pi / NFFT)
-            phase = np.stack([np.cos(angle), -np.sin(angle)], axis=1).reshape(-1) * scale
+            phase = np.stack([np.cos(angle), -np.sin(angle)], axis=0).reshape(-1) * scale
             high, mid, low = split3(phase.astype(np.float32))
             at = GROUP * (row + LEAD)
             table[window, at : at + 3, :192] = np.concatenate([high, high, mid, high, low, mid])
@@ -62,10 +63,16 @@
     return table
 
 
+def halves(first, second):
+    lanes = lax.broadcasted_iota(jnp.int32, first.shape, 1)
+    low = jnp.where(lanes < HALF, first, pltpu.roll(second, HALF, 1))
+    return low, jnp.where(lanes < HALF, pltpu.roll(first, HALF, 1), second)
+
+
 def main_product(gap_ref, recip_ref, data_ref, weights_ref, out_ref, acc_ref, mask_ref):
     step = pl.program_id(0)
     depth = data_ref.shape[3]
-    slots = out_ref.shape[0]
+    pairs = out_ref.shape[0]
 
     @pl.when(step == 0)
     def _():
@@ -73,19 +80,24 @@
         gap = jnp.where(gap_ref[...] == 1, 1.0, 0.0)
         full = jnp.concatenate([gap, jnp.zeros((RECV - NEAR, RECV), F32)], axis=0)
         mask_ref[...] = (1.0 - full.T).astype(BF16)
-        out_ref[:, RECIP_AT:GAP_AT] = jnp.broadcast_to(recip_ref[...][None], (slots, 2 * NEAR, RECV))
-        out_ref[:, GAP_AT:NEAR_AT] = jnp.broadcast_to(gap.astype(BF16)[None], (slots, NEAR, RECV))
+        recip = recip_ref[...].astype(F32)
+        recip = halves(recip[:NEAR], recip[NEAR:])
+        gaps = gap, pltpu.roll(gap, HALF, 1)
         lanes = lax.broadcasted_iota(jnp.int32, (NEAR, RECV), 1)
-        for group in range(slots * 8 // 64):
-            at = RECV * (group // 2)
+        for half in range(2):
+            out_ref[:, half, RECIP_AT:GAP_AT] = jnp.broadcast_to(
+                recip[half].astype(BF16)[None], (pairs, NEAR, RECV)
+            )
+        for group in range(pairs // 2):
+            at, off = RECV * (group // 4), 32 * (group % 4)
             real = weights_ref[0, 0, :NEAR, at : at + RECV].astype(F32)
             imag = weights_ref[1, 0, :NEAR, at : at + RECV].astype(F32)
-            if group % 2:
-                real = pltpu.roll(real, 64, 1)
-            else:
-                imag = pltpu.roll(imag, 64, 1)
-            near = jnp.where(lanes < 64, real, imag).astype(BF16)
-            out_ref[8 * group : 8 * group + 8, NEAR_AT:] = jnp.broadcast_to(near[None], (8, NEAR, RECV))
+            real = pltpu.roll(real, (HALF - off) % RECV, 1)
+            imag = pltpu.roll(imag, (HALF + 32 - off) % RECV, 1)
+            near = jnp.where(lanes < HALF + 32, real, imag)
+            for half in range(2):
+                tile = jnp.where(lanes < HALF, gaps[half], near).astype(BF16)
+                out_ref[2 * group : 2 * group + 2, half, GAP_AT:] = jnp.broadcast_to(tile[None], (2, NEAR, RECV))
 
     @pl.when(step == 1)
     def _():
@@ -97,45 +109,43 @@
     panel = jnp.concatenate([near, panel[:, RECV:]], axis=1)
     both = jnp.concatenate([weights_ref[0, 0], weights_ref[1, 0]], axis=1)
     product = jnp.dot(panel, both, preferred_element_type=F32)
-    half = product.shape[1] // 2
-    acc_ref[0] += product[:RECV, :half] - product[RECV:, half:]
-    acc_ref[1] += product[:RECV, half:] + product[RECV:, :half]
+    width = product.shape[1] // 2
+    acc_ref[0] += product[:RECV, :width] - product[RECV:, width:]
+    acc_ref[1] += product[:RECV, width:] + product[RECV:, :width]
 
     @pl.when(step == pl.num_programs(0) - 1)
     def _():
-        real = acc_ref[0].T.reshape(slots, 8, RECV)
-        imag = acc_ref[1].T.reshape(slots, 8, RECV)
-        high, low = two_parts(jnp.concatenate([real, imag], axis=1))
-        out_ref[:, :LOW_AT] = high
-        out_ref[:, LOW_AT:RECIP_AT] = low
+        for half, pred in enumerate(halves(acc_ref[0].T, acc_ref[1].T)):
+            high, low = two_parts(pred.reshape(pairs, 16, RECV))
+            out_ref[:, half, :LOW_AT] = high
+            out_ref[:, half, LOW_AT:RECIP_AT] = low
 
 
 def sum_and_fill(owner_ref, part_ref, out_ref, z_ref, w_ref, f_ref, block_ref, sem):
     slots = part_ref.shape[0]
     copy = pltpu.make_async_copy(owner_ref, block_ref, sem)
     copy.start()
-    place = lax.rem(lax.axis_index("src"), 8)
+    place = lax.rem(lax.axis_index("pair"), 2)
     total = jnp.zeros((16, RECV), F32)
     for j in range(slots):
         total = total + part_ref[j, :LOW_AT].astype(F32) + part_ref[j, LOW_AT:RECIP_AT].astype(F32)
     copy.wait()
+    lanes = lax.broadcasted_iota(jnp.int32, (NEAR, RECV), 1)
     for j in range(slots):
-        block = block_ref[j]
-        gap = part_ref[block, GAP_AT:NEAR_AT]
+        tile = part_ref[block_ref[j], GAP_AT:]
+        gap = tile.astype(F32)
+        gap = jnp.where(lanes < HALF, gap, pltpu.roll(gap, HALF, 1))
         at = slice(NEAR * j, NEAR * j + NEAR)
-        z_ref[at, :RECV] = part_ref[j, RECIP_AT : RECIP_AT + NEAR] * gap
-        z_ref[at, RECV:] = part_ref[j, RECIP_AT + NEAR : GAP_AT] * gap
-        w_ref[at, :] = part_ref[block, NEAR_AT:]
+        z_ref[at, :] = (part_ref[j, RECIP_AT:GAP_AT].astype(F32) * gap).astype(BF16)
+        w_ref[at, :] = tile
     f_ref[...] = lax.dot_general(
         w_ref[...], z_ref[...], (((0,), (0,)), ((), ())), preferred_element_type=F32
     )
-    at = pl.multiple_of(place * 8, 8)
-    by_real = f_ref[pl.ds(at, 8), :]
-    by_imag = f_ref[pl.ds(at + 64, 8), :]
-    real = total[:8] + by_real[:, :RECV] - by_imag[:, RECV:]
-    imag = total[8:] + by_imag[:, :RECV] + by_real[:, RECV:]
-    out_ref[:, :8] = jnp.broadcast_to(real[None], (out_ref.shape[0], 8, RECV))
-    out_ref[:, 8:] = jnp.broadcast_to(imag[None], (out_ref.shape[0], 8, RECV))
+    at = pl.multiple_of(HALF + place * 16, 16)
+    by_real = f_ref[pl.ds(at, 16), :]
+    by_imag = pltpu.roll(f_ref[pl.ds(at + 32, 16), :], HALF, 1)
+    pred = total + by_real + jnp.where(lanes < HALF, -by_imag, by_imag)
+    out_ref[...] = jnp.broadcast_to(pred.reshape(1, 2, 8, RECV), out_ref.shape)
 
 
 def two_parts(x):
@@ -145,7 +155,11 @@
 
 def trace_and_gram(keep_ref, x_ref, rows_ref, target_ref, gram_ref, trace_ref, a_ref, g_ref):
     sources = 8
-    x = jnp.concatenate([x_ref[pl.ds(s, 2 * NF, stride=sources), :] for s in range(sources)], axis=1)
+    columns = []
+    for s in range(sources):
+        low, high = (x_ref[pl.ds(8 * half + s, NF, stride=16), :] for half in range(2))
+        columns.append(jnp.concatenate(halves(low, high), axis=0))
+    x = jnp.concatenate(columns, axis=1)
     high, rest = x.astype(BF16), x
     rest = rest - high.astype(F32)
     mid = rest.astype(BF16)
@@ -262,7 +276,8 @@
 
 def body(data, recip, gap, owner, weights, start_row, end_row, recorded):
     freq_here = lax.axis_index("freq")
-    src_count = lax.axis_size("src")
+    src_count = lax.axis_size("pair") * lax.axis_size("half")
+    pairs = src_count // 2
     total_out = weights.shape[3]
     points = data.shape[3]
 
@@ -271,32 +286,34 @@
     parts = pl.pallas_call(
         main_product,
         grid=(points // depth,),
-        out_shape=jax.ShapeDtypeStruct((src_count, SLOT_ROWS, RECV), BF16),
+        out_shape=jax.ShapeDtypeStruct((pairs, 2, SLOT_ROWS, RECV), BF16),
         in_specs=[
             pl.BlockSpec((NEAR, RECV), lambda k: (0, 0)),
             pl.BlockSpec((2 * NEAR, RECV), lambda k: (0, 0)),
             pl.BlockSpec((2, 1, RECV, depth), lambda k: (0, 0, 0, k)),
             pl.BlockSpec((2, 1, depth, total_out), lambda k: (0, 0, k, 0)),
         ],
-        out_specs=pl.BlockSpec((src_count, SLOT_ROWS, RECV), lambda k: (0, 0, 0)),
+        out_specs=pl.BlockSpec((pairs, 2, SLOT_ROWS, RECV), lambda k: (0, 0, 0, 0)),
         scratch_shapes=[pltpu.VMEM((2, RECV, total_out), F32), pltpu.VMEM((RECV, RECV), BF16)],
         cost_estimate=pl.CostEstimate(flops=8 * RECV * points * total_out, bytes_accessed=5000000, transcendentals=0),
     )(gap.T, recip_rows, data, weights)
-    parts = lax.all_to_all(parts, "src", 0, 0, tiled=True)
+    parts = parts.reshape(src_count, SLOT_ROWS, RECV)
+    parts = lax.all_to_all(parts, ("pair", "half"), 0, 0, tiled=True)
     copies = call(
         sum_and_fill,
-        jax.ShapeDtypeStruct((NF, 16, RECV), F32),
+        jax.ShapeDtypeStruct((NF, 2, 8, RECV), F32),
         (owner, parts),
         [pl.BlockSpec(memory_space=pl.ANY), VMEM],
         [
-            pltpu.VMEM((NEAR * src_count, 2 * RECV), BF16),
             pltpu.VMEM((NEAR * src_count, RECV), BF16),
-            pltpu.VMEM((RECV, 2 * RECV), F32),
+            pltpu.VMEM((NEAR * src_count, RECV), BF16),
+            pltpu.VMEM((RECV, RECV), F32),
             pltpu.SMEM((src_count,), jnp.int32),
             pltpu.SemaphoreType.DMA,
         ],
     )
-    spread = lax.all_to_all(copies, "freq", 0, 0, tiled=True).reshape(NF * 16, RECV)
+    copies = copies.reshape(NF * 2, 8, RECV)
+    spread = lax.all_to_all(copies, ("freq", "half"), 0, 0, tiled=True).reshape(NF * 16, RECV)
 
     begin = freq_here * T_DEV - HALO
     first, last = start_row[0] - begin, end_row[0] - begin
@@ -315,7 +332,7 @@
         [VMEM] * 4,
         [pltpu.VMEM((8 * GROWS, RECV), F32), pltpu.VMEM((GROWS, GROWS), F32)],
     )
-    gram = lax.all_to_all(gram, "src", 0, 0, tiled=True)
+    gram = lax.all_to_all(gram, ("pair", "half"), 0, 0, tiled=True)
     damping = float(WROWS * total_out * RECV)
     primaries, filters = call(
         functools.partial(solve_and_filter, damping),
@@ -328,20 +345,23 @@
 
 
 def solution(mesh):
+    freq, src = mesh.devices.shape
+    mesh = Mesh(mesh.devices.reshape(freq, src // 2, 2), ("freq", "pair", "half"))
+    src = ("pair", "half")
     placed = (
-        P(None, "freq", None, "src"),
-        P(None, "freq", None, "src"),
-        P(None, "src"),
+        P(None, "freq", None, src),
+        P(None, "freq", None, src),
+        P(None, src),
         P(),
-        P(None, "freq", "src", None),
+        P(None, "freq", src, None),
         P("freq"),
         P("freq"),
-        P("freq", "src", None),
+        P("freq", src, None),
     )
     return jax.shard_map(
         body,
         mesh=mesh,
         in_specs=placed,
-        out_specs=(P("freq", "src", None), P("freq", None)),
+        out_specs=(P("freq", src, None), P("freq", None)),
         check_vma=False,
     )

time: 78.9 us -> 74.3 us (0.942)
  waiting for transfers between devices: 29.5 us -> 24.4 us
  starting transfers between devices: 20.7 us -> 22.1 us
  blocking collectives: 15.4 us -> 14.3 us
    all_to_all x2, waiting for transfers between devices: 29.5 us -> 24.4 us  [the longest x1 16.3 us: body(): parts = lax.all_to_all(parts, ('pair', 'half'), 0, 0, tiled=True)]
    all_to_all x2, starting transfers between devices: 20.7 us -> 22.1 us  [the longest x1 11.9 us: body(): lax.all_to_all(copies, ('freq', 'half'), 0, 0, tiled=True)]
    all_to_all x1, blocking collectives: 15.4 us -> 14.3 us  [body(): gram = lax.all_to_all(gram, ('pair', 'half'), 0, 0, tiled=True)]
where the time goes in v4:
time: 74.3 us; the launch traced here: 73.9 us
  waiting for transfers between devices  24.4 us (33%)
  starting transfers between devices  22.1 us (30%)
  blocking collectives  14.3 us (19%)
  Pallas kernels  9.9 us (13%)
  between operations  2.02 us (3%)
  other arithmetic  1.02 us (1%)
    all_to_all x1, waiting for transfers between devices, body(): parts = lax.all_to_all(parts, ('pair', 'half'), 0, 0, tiled=True)  16.3 us
    all_to_all x1, blocking collectives, body(): gram = lax.all_to_all(gram, ('pair', 'half'), 0, 0, tiled=True)  14.3 us
    all_to_all x1, starting transfers between devices, body(): lax.all_to_all(copies, ('freq', 'half'), 0, 0, tiled=True)  11.9 us
    all_to_all x1, starting transfers between devices, body(): parts = lax.all_to_all(parts, ('pair', 'half'), 0, 0, tiled=True)  10.2 us
    all_to_all x1, waiting for transfers between devices, body(): lax.all_to_all(copies, ('freq', 'half'), 0, 0, tiled=True)  8.11 us
    pallas_call x3, Pallas kernels, call(): pl.pallas_call(kernel, out_shape=out_shape, in_specs=specs, out_specs=jax...  5.83 us
    pallas_call x1, Pallas kernels, body(): pl.pallas_call(main_product, grid=(points // depth,), out_shape=jax.Shape...  4.08 us
  transfers between devices with their start and end apart: 2, of which 2 were waited for; matrix products, arithmetic and copies ran while one was open for 1% of the time, Pallas kernels for 0%

profile of v4, /device:TPU:8, one launch (start us, length us, event | category | flops | bytes accessed | tf_op | source)
XLA Modules:
  0.0 73.9 jit_solution(17196411135345010268)
XLA Ops:
  0.6 0.0 copy-start.1
  0.6 0.0 copy-start
  0.7 4.1 %shard_map.104 = bf16[16,2,64,128]{3,2,1,0:T(8,128)(2,1)} custom-call(s32[16,128]{1,0:T(8,128)} %bitcast.23, bf16[32,128]{1,0:T(8,128)(2,1)} %bitcast.24, bf16[2,1,128,3072]{3,2,1,0:T(8,128)(2,1)} %data_ref.1, bf16[2,1,3072,256]{3,2,1,0:T(8,128)(2,1)} %weights_ref.1), custom_call_target="tpu_custom_call" | custom-call | flops 805306368 | bytes 5000000 | tf_op jit(solution)/shard_map/pallas_call | solution.py:286
  4.7 10.2 %all-to-all-start = ((bf16[32,64,128]{2,1,0:T(8,128)(2,1)}), bf16[32,64,128]{2,1,0:T(8,128)(2,1)S(1)}, u32[]{:S(2)}, u32[]{:S(2)}) async-start(bf16[32,64,128]{2,1,0:T(8,128)(2,1)} %bitcast.21), calls=%async_computation | async-start | bytes 1048576 | tf_op jit(solution)/shard_map/all_to_all | solution.py:301
  16.2 16.3 %all-to-all-done.part_ref = bf16[32,64,128]{2,1,0:T(8,128)(2,1)S(1)} async-done(((bf16[32,64,128]{2,1,0:T(8,128)(2,1)}), bf16[32,64,128]{2,1,0:T(8,128)(2,1)S(1)}, u32[]{:S(2)}, u32[]{:S(2)}) %all-to-all-start) | async-done | bytes 524320 | tf_op jit(solution)/shard_map/all_to_all | solution.py:301
  32.5 0.0 copy-done.1
  32.5 1.6 %shard_map.105 = f32[16,2,8,128]{3,2,1,0:T(8,128)} custom-call(s32[32]{0:T(128)S(1)} %copy-done.1, bf16[32,64,128]{2,1,0:T(8,128)(2,1)S(1)} %all-to-all-done.part_ref), custom_call_target="tpu_custom_call" | custom-call | flops 1000000 | bytes 1000000 | tf_op jit(solution)/shard_map/pallas_call | solution.py:266
  34.1 11.9 %all-to-all-start.1 = ((f32[32,8,128]{2,1,0:T(8,128)}), f32[32,8,128]{2,1,0:T(8,128)S(1)}, u32[]{:S(2)}, u32[]{:S(2)}) async-start(f32[32,8,128]{2,1,0:T(8,128)} %bitcast.7), calls=%async_computation.1 | async-start | bytes 262144 | tf_op jit(solution)/shard_map/all_to_all | solution.py:316
  46.1 0.0 copy-done
  46.1 1.0 %bitcast_select_fusion.rows_ref = bf16[256,256]{1,0:T(8,128)(2,1)S(1)} fusion(bf16[16,256,256]{2,1,0:T(8,128)(2,1)} %constant.43.clone, s32[]{:T(128)S(6)} %select_n.20, pred[256]{0:T(512)(128)(4,1)S(1)} %compare_and_fusion), kind=kLoop, calls=%fused_computation | loop fusion | flops 65536 | bytes 262404 | tf_op jit(solution)/shard_map/jit(_where)/select_n | solution.py:325
  47.2 8.1 %all-to-all-done.1 = f32[32,8,128]{2,1,0:T(8,128)S(1)} async-done(((f32[32,8,128]{2,1,0:T(8,128)}), f32[32,8,128]{2,1,0:T(8,128)S(1)}, u32[]{:S(2)}, u32[]{:S(2)}) %all-to-all-start.1) | async-done | bytes 131104 | tf_op jit(solution)/shard_map/all_to_all | solution.py:316
  55.3 0.1 iota.17.keep_ref
  55.3 1.6 %shard_map.106 = (f32[32,8,128]{2,1,0:T(8,128)S(1)}, f32[448,128]{1,0:T(8,128)S(1)}) custom-call(f32[48,128]{1,0:T(8,128)S(1)} %iota.17.keep_ref, f32[256,128]{1,0:T(8,128)S(1)} %bitcast.19, bf16[256,256]{1,0:T(8,128)(2,1)S(1)} %bitcast_select_fusion.rows_ref, bf16[64,1024]{1,0:T(8,128)(2,1)S(1)} %pad.4.target_ref), custom_call_target="tpu_custom_call" | custom-call | flops 1000000 | bytes 1000000 | tf_op jit(solution)/shard_map/pallas_call | solution.py:266
  57.0 14.3 %all_to_all.15.gram_ref = f32[32,8,128]{2,1,0:T(8,128)S(1)} all-to-all(f32[32,8,128]{2,1,0:T(8,128)S(1)} %get-tuple-element.4), channel_id=1, replica_groups=mesh['freq'=16,'pair'=16,'half'=2] {'pair','half'}, dimensions={0} | all-to-all | bytes 262144 | tf_op jit(solution)/shard_map/all_to_all | solution.py:335
  71.3 2.6 %shard_map.107 = (bf16[48,8,128]{2,1,0:T(8,128)(2,1)}, f32[1,27]{1,0:T(1,128)}) custom-call(f32[48,128]{1,0:T(8,128)S(1)} %iota.17.keep_ref, f32[32,8,128]{2,1,0:T(8,128)S(1)} %all_to_all.15.gram_ref, f32[448,128]{1,0:T(8,128)S(1)} %get-tuple-element.5.trace_ref, bf16[48,8,128]{2,1,0:T(8,128)(2,1)S(1)} %copy-done), custom_call_target="tpu_custom_call" | custom-call | flops 1000000 | bytes 1000000 | tf_op jit(solution)/shard_map/pallas_call | solution.py:266
  (4 shorter events, 0.0 us)
Async XLA Ops:
  0.6 31.9 %copy-start.1 = (s32[32]{0:T(128)S(1)}, s32[32]{0:T(128)}, u32[]{:S(2)}) copy-start(s32[32]{0:T(128)} %owner_ref.1) | copy-start | bytes 388
  0.6 45.4 %copy-start = (bf16[48,8,128]{2,1,0:T(8,128)(2,1)S(1)}, bf16[48,8,128]{2,1,0:T(8,128)(2,1)}, u32[]{:S(2)}) copy-start(bf16[48,8,128]{2,1,0:T(8,128)(2,1)} %recorded_ref.1) | copy-start | bytes 294916
  4.7 27.8 %all-to-all-start = ((bf16[32,64,128]{2,1,0:T(8,128)(2,1)}), bf16[32,64,128]{2,1,0:T(8,128)(2,1)S(1)}, u32[]{:S(2)}, u32[]{:S(2)}) async-start(bf16[32,64,128]{2,1,0:T(8,128)(2,1)} %bitcast.21), calls=%async_computation | async-start | bytes 1048576 | tf_op jit(solution)/shard_map/all_to_all | solution.py:301
  34.1 21.1 %all-to-all-start.1 = ((f32[32,8,128]{2,1,0:T(8,128)}), f32[32,8,128]{2,1,0:T(8,128)S(1)}, u32[]{:S(2)}, u32[]{:S(2)}) async-start(f32[32,8,128]{2,1,0:T(8,128)} %bitcast.7), calls=%async_computation.1 | async-start | bytes 262144 | tf_op jit(solution)/shard_map/all_to_all | solution.py:316

commit v5 on v4

--- a/solution.py
+++ b/solution.py
@@ -121,18 +121,15 @@
             out_ref[:, half, LOW_AT:RECIP_AT] = low
 
 
-def sum_and_fill(owner_ref, part_ref, out_ref, z_ref, w_ref, f_ref, block_ref, sem):
+def sum_and_fill(owner_ref, part_ref, out_ref, z_ref, w_ref, f_ref):
     slots = part_ref.shape[0]
-    copy = pltpu.make_async_copy(owner_ref, block_ref, sem)
-    copy.start()
     place = lax.rem(lax.axis_index("pair"), 2)
     total = jnp.zeros((16, RECV), F32)
     for j in range(slots):
         total = total + part_ref[j, :LOW_AT].astype(F32) + part_ref[j, LOW_AT:RECIP_AT].astype(F32)
-    copy.wait()
     lanes = lax.broadcasted_iota(jnp.int32, (NEAR, RECV), 1)
     for j in range(slots):
-        tile = part_ref[block_ref[j], GAP_AT:]
+        tile = part_ref[owner_ref[0, j], GAP_AT:]
         gap = tile.astype(F32)
         gap = jnp.where(lanes < HALF, gap, pltpu.roll(gap, HALF, 1))
         at = slice(NEAR * j, NEAR * j + NEAR)
@@ -302,14 +299,12 @@
     copies = call(
         sum_and_fill,
         jax.ShapeDtypeStruct((NF, 2, 8, RECV), F32),
-        (owner, parts),
-        [pl.BlockSpec(memory_space=pl.ANY), VMEM],
+        (owner.reshape(1, src_count), parts),
+        [VMEM, VMEM],
         [
             pltpu.VMEM((NEAR * src_count, RECV), BF16),
             pltpu.VMEM((NEAR * src_count, RECV), BF16),
             pltpu.VMEM((RECV, RECV), F32),
-            pltpu.SMEM((src_count,), jnp.int32),
-            pltpu.SemaphoreType.DMA,
         ],
     )
     copies = copies.reshape(NF * 2, 8, RECV)

time: 74.3 us -> 73.8 us (level)
  no operation moved by 1% of the time
where the time goes in v5:
time: 73.8 us; the launch traced here: 73.5 us
  waiting for transfers between devices  24.4 us (33%)
  starting transfers between devices  22.1 us (30%)
  blocking collectives  14.3 us (19%)
  Pallas kernels  9.48 us (13%)
  between operations  2.02 us (3%)
  other arithmetic  1.02 us (1%)
    all_to_all x1, waiting for transfers between devices, body(): parts = lax.all_to_all(parts, ('pair', 'half'), 0, 0, tiled=True)  16.3 us
    all_to_all x1, blocking collectives, body(): gram = lax.all_to_all(gram, ('pair', 'half'), 0, 0, tiled=True)  14.3 us
    all_to_all x1, starting transfers between devices, body(): lax.all_to_all(copies, ('freq', 'half'), 0, 0, tiled=True)  11.9 us
    all_to_all x1, starting transfers between devices, body(): parts = lax.all_to_all(parts, ('pair', 'half'), 0, 0, tiled=True)  10.2 us
    all_to_all x1, waiting for transfers between devices, body(): lax.all_to_all(copies, ('freq', 'half'), 0, 0, tiled=True)  8.11 us
    pallas_call x3, Pallas kernels, call(): pl.pallas_call(kernel, out_shape=out_shape, in_specs=specs, out_specs=jax...  5.41 us
    pallas_call x1, Pallas kernels, body(): pl.pallas_call(main_product, grid=(points // depth,), out_shape=jax.Shape...  4.08 us
  transfers between devices with their start and end apart: 2, of which 2 were waited for; matrix products, arithmetic and copies ran while one was open for 1% of the time, Pallas kernels for 0%

profile of v5, /device:TPU:8, one launch (start us, length us, event | category | flops | bytes accessed | tf_op | source)
XLA Modules:
  0.0 73.5 jit_solution(10717683412189528293)
XLA Ops:
  0.6 0.0 copy-start.1
  0.6 0.0 copy-start
  0.7 4.1 %shard_map.104 = bf16[16,2,64,128]{3,2,1,0:T(8,128)(2,1)} custom-call(s32[16,128]{1,0:T(8,128)} %bitcast.25, bf16[32,128]{1,0:T(8,128)(2,1)} %bitcast.26, bf16[2,1,128,3072]{3,2,1,0:T(8,128)(2,1)} %data_ref.1, bf16[2,1,3072,256]{3,2,1,0:T(8,128)(2,1)} %weights_ref.1), custom_call_target="tpu_custom_call" | custom-call | flops 805306368 | bytes 5000000 | tf_op jit(solution)/shard_map/pallas_call | solution.py:283
  4.7 10.2 %all-to-all-start = ((bf16[32,64,128]{2,1,0:T(8,128)(2,1)}), bf16[32,64,128]{2,1,0:T(8,128)(2,1)S(1)}, u32[]{:S(2)}, u32[]{:S(2)}) async-start(bf16[32,64,128]{2,1,0:T(8,128)(2,1)} %bitcast.23), calls=%async_computation | async-start | bytes 1048576 | tf_op jit(solution)/shard_map/all_to_all | solution.py:298
  16.2 16.3 %all-to-all-done.part_ref = bf16[32,64,128]{2,1,0:T(8,128)(2,1)S(1)} async-done(((bf16[32,64,128]{2,1,0:T(8,128)(2,1)}), bf16[32,64,128]{2,1,0:T(8,128)(2,1)S(1)}, u32[]{:S(2)}, u32[]{:S(2)}) %all-to-all-start) | async-done | bytes 524320 | tf_op jit(solution)/shard_map/all_to_all | solution.py:298
  32.5 0.0 copy-done.1
  32.5 1.2 %shard_map.105 = f32[16,2,8,128]{3,2,1,0:T(8,128)} custom-call(s32[1,32]{1,0:T(1,128)S(1)} %bitcast.22, bf16[32,64,128]{2,1,0:T(8,128)(2,1)S(1)} %all-to-all-done.part_ref), custom_call_target="tpu_custom_call" | custom-call | flops 1000000 | bytes 1000000 | tf_op jit(solution)/shard_map/pallas_call | solution.py:263
  33.7 11.9 %all-to-all-start.1 = ((f32[32,8,128]{2,1,0:T(8,128)}), f32[32,8,128]{2,1,0:T(8,128)S(1)}, u32[]{:S(2)}, u32[]{:S(2)}) async-start(f32[32,8,128]{2,1,0:T(8,128)} %bitcast.8), calls=%async_computation.1 | async-start | bytes 262144 | tf_op jit(solution)/shard_map/all_to_all | solution.py:311
  45.6 0.0 copy-done
  45.7 1.0 %bitcast_select_fusion.rows_ref = bf16[256,256]{1,0:T(8,128)(2,1)S(1)} fusion(bf16[16,256,256]{2,1,0:T(8,128)(2,1)} %constant.43.clone, s32[]{:T(128)S(6)} %select_n.20, pred[256]{0:T(512)(128)(4,1)S(1)} %compare_and_fusion), kind=kLoop, calls=%fused_computation | loop fusion | flops 65536 | bytes 262404 | tf_op jit(solution)/shard_map/jit(_where)/select_n | solution.py:320
  46.7 8.1 %all-to-all-done.1 = f32[32,8,128]{2,1,0:T(8,128)S(1)} async-done(((f32[32,8,128]{2,1,0:T(8,128)}), f32[32,8,128]{2,1,0:T(8,128)S(1)}, u32[]{:S(2)}, u32[]{:S(2)}) %all-to-all-start.1) | async-done | bytes 131104 | tf_op jit(solution)/shard_map/all_to_all | solution.py:311
  54.8 0.1 iota.17.keep_ref
  54.9 1.6 %shard_map.106 = (f32[32,8,128]{2,1,0:T(8,128)S(1)}, f32[448,128]{1,0:T(8,128)S(1)}) custom-call(f32[48,128]{1,0:T(8,128)S(1)} %iota.17.keep_ref, f32[256,128]{1,0:T(8,128)S(1)} %bitcast.20, bf16[256,256]{1,0:T(8,128)(2,1)S(1)} %bitcast_select_fusion.rows_ref, bf16[64,1024]{1,0:T(8,128)(2,1)S(1)} %pad.4.target_ref), custom_call_target="tpu_custom_call" | custom-call | flops 1000000 | bytes 1000000 | tf_op jit(solution)/shard_map/pallas_call | solution.py:263
  56.5 14.3 %all_to_all.15.gram_ref = f32[32,8,128]{2,1,0:T(8,128)S(1)} all-to-all(f32[32,8,128]{2,1,0:T(8,128)S(1)} %get-tuple-element.4), channel_id=1, replica_groups=mesh['freq'=16,'pair'=16,'half'=2] {'pair','half'}, dimensions={0} | all-to-all | bytes 262144 | tf_op jit(solution)/shard_map/all_to_all | solution.py:330
  70.9 2.6 %shard_map.107 = (bf16[48,8,128]{2,1,0:T(8,128)(2,1)}, f32[1,27]{1,0:T(1,128)}) custom-call(f32[48,128]{1,0:T(8,128)S(1)} %iota.17.keep_ref, f32[32,8,128]{2,1,0:T(8,128)S(1)} %all_to_all.15.gram_ref, f32[448,128]{1,0:T(8,128)S(1)} %get-tuple-element.5.trace_ref, bf16[48,8,128]{2,1,0:T(8,128)(2,1)S(1)} %copy-done), custom_call_target="tpu_custom_call" | custom-call | flops 1000000 | bytes 1000000 | tf_op jit(solution)/shard_map/pallas_call | solution.py:263
  (4 shorter events, 0.0 us)
Async XLA Ops:
  0.6 31.9 %copy-start.1 = (s32[32]{0:T(128)S(1)}, s32[32]{0:T(128)}, u32[]{:S(2)}) copy-start(s32[32]{0:T(128)} %param.12) | copy-start | bytes 388
  0.6 45.0 %copy-start = (bf16[48,8,128]{2,1,0:T(8,128)(2,1)S(1)}, bf16[48,8,128]{2,1,0:T(8,128)(2,1)}, u32[]{:S(2)}) copy-start(bf16[48,8,128]{2,1,0:T(8,128)(2,1)} %recorded_ref.1) | copy-start | bytes 294916
  4.7 27.8 %all-to-all-start = ((bf16[32,64,128]{2,1,0:T(8,128)(2,1)}), bf16[32,64,128]{2,1,0:T(8,128)(2,1)S(1)}, u32[]{:S(2)}, u32[]{:S(2)}) async-start(bf16[32,64,128]{2,1,0:T(8,128)(2,1)} %bitcast.23), calls=%async_computation | async-start | bytes 1048576 | tf_op jit(solution)/shard_map/all_to_all | solution.py:298
  33.7 21.1 %all-to-all-start.1 = ((f32[32,8,128]{2,1,0:T(8,128)}), f32[32,8,128]{2,1,0:T(8,128)S(1)}, u32[]{:S(2)}, u32[]{:S(2)}) async-start(f32[32,8,128]{2,1,0:T(8,128)} %bitcast.8), calls=%async_computation.1 | async-start | bytes 262144 | tf_op jit(solution)/shard_map/all_to_all | solution.py:311

commit v6 on v5

--- a/solution.py
+++ b/solution.py
@@ -28,8 +28,10 @@
 TARGET_COL = GROUP * LEAD + 3
 CENTRE_ROW = GROUP * LEAD + 1
 PACK_AT = (0, 40, 72, 96, 112)
-LOW_AT, RECIP_AT, GAP_AT, SLOT_ROWS = 16, 32, 48, 64
+RECIP_AT, GAP_AT, SLOT_ROWS = 16, 32, 48
 HALF = RECV // 2
+IMAG_AT, SCALE_AT = HALF + 16, HALF + 32
+SPAN = 166.0
 VMEM = pl.BlockSpec(memory_space=pltpu.VMEM)
 F32 = jnp.float32
 BF16 = jnp.bfloat16
@@ -69,7 +71,17 @@
     return low, jnp.where(lanes < HALF, pltpu.roll(first, HALF, 1), second)
 
 
-def main_product(gap_ref, recip_ref, data_ref, weights_ref, out_ref, acc_ref, mask_ref):
+def encode(value, scale):
+    size = jnp.exp(jnp.abs(value) * (SPAN / scale) - SPAN / 2)
+    return jnp.where(value < 0, -size, size)
+
+
+def decode(code, scale):
+    size = (jnp.log(jnp.abs(code)) + SPAN / 2) * (scale * (1.0 / SPAN))
+    return jnp.where(code < 0, -size, size)
+
+
+def main_product(gap_ref, recip_ref, data_ref, weights_ref, out_ref, acc_ref, mask_ref, near_ref):
     step = pl.program_id(0)
     depth = data_ref.shape[3]
     pairs = out_ref.shape[0]
@@ -82,22 +94,18 @@
         mask_ref[...] = (1.0 - full.T).astype(BF16)
         recip = recip_ref[...].astype(F32)
         recip = halves(recip[:NEAR], recip[NEAR:])
-        gaps = gap, pltpu.roll(gap, HALF, 1)
         lanes = lax.broadcasted_iota(jnp.int32, (NEAR, RECV), 1)
         for half in range(2):
             out_ref[:, half, RECIP_AT:GAP_AT] = jnp.broadcast_to(
                 recip[half].astype(BF16)[None], (pairs, NEAR, RECV)
             )
-        for group in range(pairs // 2):
-            at, off = RECV * (group // 4), 32 * (group % 4)
+        for pair in range(pairs):
+            at, off = RECV * (pair // 8), 16 * (pair % 8)
             real = weights_ref[0, 0, :NEAR, at : at + RECV].astype(F32)
             imag = weights_ref[1, 0, :NEAR, at : at + RECV].astype(F32)
             real = pltpu.roll(real, (HALF - off) % RECV, 1)
-            imag = pltpu.roll(imag, (HALF + 32 - off) % RECV, 1)
-            near = jnp.where(lanes < HALF + 32, real, imag)
-            for half in range(2):
-                tile = jnp.where(lanes < HALF, gaps[half], near).astype(BF16)
-                out_ref[2 * group : 2 * group + 2, half, GAP_AT:] = jnp.broadcast_to(tile[None], (2, NEAR, RECV))
+            imag = pltpu.roll(imag, (IMAG_AT - off) % RECV, 1)
+            near_ref[pair] = jnp.where(lanes < IMAG_AT, real, imag)
 
     @pl.when(step == 1)
     def _():
@@ -115,18 +123,26 @@
 
     @pl.when(step == pl.num_programs(0) - 1)
     def _():
+        gap = jnp.where(gap_ref[...] == 1, 1.0, 0.0)
+        gaps = gap, pltpu.roll(gap, HALF, 1)
+        lanes = lax.broadcasted_iota(jnp.int32, (pairs, NEAR, RECV), 2)
         for half, pred in enumerate(halves(acc_ref[0].T, acc_ref[1].T)):
-            high, low = two_parts(pred.reshape(pairs, 16, RECV))
-            out_ref[:, half, :LOW_AT] = high
-            out_ref[:, half, LOW_AT:RECIP_AT] = low
+            pred = pred.reshape(pairs, 16, RECV)
+            scale = jnp.max(jnp.abs(pred), axis=(1, 2), keepdims=True) * 1.01 + 1e-30
+            scale = scale.astype(BF16).astype(F32)
+            out_ref[:, half, :RECIP_AT] = encode(pred, scale).astype(BF16)
+            tile = jnp.where(lanes < SCALE_AT, near_ref[...], jnp.broadcast_to(scale, lanes.shape))
+            tile = jnp.where(lanes < HALF, jnp.broadcast_to(gaps[half][None], lanes.shape), tile)
+            out_ref[:, half, GAP_AT:] = tile.astype(BF16)
 
 
 def sum_and_fill(owner_ref, part_ref, out_ref, z_ref, w_ref, f_ref):
     slots = part_ref.shape[0]
-    place = lax.rem(lax.axis_index("pair"), 2)
     total = jnp.zeros((16, RECV), F32)
     for j in range(slots):
-        total = total + part_ref[j, :LOW_AT].astype(F32) + part_ref[j, LOW_AT:RECIP_AT].astype(F32)
+        scale = part_ref[j, GAP_AT:].astype(F32)[:, SCALE_AT : SCALE_AT + 1]
+        code = part_ref[j, :RECIP_AT].astype(F32)
+        total = total + decode(code, jnp.broadcast_to(scale, code.shape))
     lanes = lax.broadcasted_iota(jnp.int32, (NEAR, RECV), 1)
     for j in range(slots):
         tile = part_ref[owner_ref[0, j], GAP_AT:]
@@ -138,9 +154,8 @@
     f_ref[...] = lax.dot_general(
         w_ref[...], z_ref[...], (((0,), (0,)), ((), ())), preferred_element_type=F32
     )
-    at = pl.multiple_of(HALF + place * 16, 16)
-    by_real = f_ref[pl.ds(at, 16), :]
-    by_imag = pltpu.roll(f_ref[pl.ds(at + 32, 16), :], HALF, 1)
+    by_real = f_ref[HALF:IMAG_AT, :]
+    by_imag = pltpu.roll(f_ref[IMAG_AT:SCALE_AT, :], HALF, 1)
     pred = total + by_real + jnp.where(lanes < HALF, -by_imag, by_imag)
     out_ref[...] = jnp.broadcast_to(pred.reshape(1, 2, 8, RECV), out_ref.shape)
 
@@ -291,7 +306,11 @@
             pl.BlockSpec((2, 1, depth, total_out), lambda k: (0, 0, k, 0)),
         ],
         out_specs=pl.BlockSpec((pairs, 2, SLOT_ROWS, RECV), lambda k: (0, 0, 0, 0)),
-        scratch_shapes=[pltpu.VMEM((2, RECV, total_out), F32), pltpu.VMEM((RECV, RECV), BF16)],
+        scratch_shapes=[
+            pltpu.VMEM((2, RECV, total_out), F32),
+            pltpu.VMEM((RECV, RECV), BF16),
+            pltpu.VMEM((pairs, NEAR, RECV), F32),
+        ],
         cost_estimate=pl.CostEstimate(flops=8 * RECV * points * total_out, bytes_accessed=5000000, transcendentals=0),
     )(gap.T, recip_rows, data, weights)
     parts = parts.reshape(src_count, SLOT_ROWS, RECV)
@@ -299,7 +318,7 @@
     copies = call(
         sum_and_fill,
         jax.ShapeDtypeStruct((NF, 2, 8, RECV), F32),
-        (owner.reshape(1, src_count), parts),
+        (jnp.broadcast_to(owner[None], (8, src_count)), parts),
         [VMEM, VMEM],
         [
             pltpu.VMEM((NEAR * src_count, RECV), BF16),

time: 73.8 us -> 71.1 us (0.963)
  waiting for transfers between devices: 24.4 us -> 21.7 us
    all_to_all x1, waiting for transfers between devices: 16.3 us -> 13.6 us  [body(): parts = lax.all_to_all(parts, ('pair', 'half'), 0, 0, tiled=True)]
where the time goes in v6:
time: 71.1 us; the launch traced here: 70.8 us
  starting transfers between devices  22.1 us (31%)
  waiting for transfers between devices  21.7 us (31%)
  blocking collectives  14.2 us (20%)
  Pallas kernels  9.6 us (14%)
  between operations  2.02 us (3%)
  other arithmetic  1.02 us (1%)
    all_to_all x1, blocking collectives, body(): gram = lax.all_to_all(gram, ('pair', 'half'), 0, 0, tiled=True)  14.2 us
    all_to_all x1, waiting for transfers between devices, body(): parts = lax.all_to_all(parts, ('pair', 'half'), 0, 0, tiled=True)  13.6 us
    all_to_all x1, starting transfers between devices, body(): lax.all_to_all(copies, ('freq', 'half'), 0, 0, tiled=True)  11.9 us
    all_to_all x1, starting transfers between devices, body(): parts = lax.all_to_all(parts, ('pair', 'half'), 0, 0, tiled=True)  10.2 us
    all_to_all x1, waiting for transfers between devices, body(): lax.all_to_all(copies, ('freq', 'half'), 0, 0, tiled=True)  8.11 us
    pallas_call x3, Pallas kernels, call(): pl.pallas_call(kernel, out_shape=out_shape, in_specs=specs, out_specs=jax...  5.39 us
    pallas_call x1, Pallas kernels, body(): pl.pallas_call(main_product, grid=(points // depth,), out_shape=jax.Shape...  4.21 us
  transfers between devices with their start and end apart: 2, of which 2 were waited for; matrix products, arithmetic and copies ran while one was open for 1% of the time, Pallas kernels for 0%

profile of v6, /device:TPU:8, one launch (start us, length us, event | category | flops | bytes accessed | tf_op | source)
XLA Modules:
  0.0 70.8 jit_solution(11576463919123091183)
XLA Ops:
  0.6 0.0 copy-start.1
  0.6 0.0 copy-start
  0.7 4.2 %shard_map.104 = bf16[16,2,48,128]{3,2,1,0:T(8,128)(2,1)} custom-call(s32[16,128]{1,0:T(8,128)} %bitcast.23, bf16[32,128]{1,0:T(8,128)(2,1)} %bitcast.24, bf16[2,1,128,3072]{3,2,1,0:T(8,128)(2,1)} %data_ref.1, bf16[2,1,3072,256]{3,2,1,0:T(8,128)(2,1)} %weights_ref.1), custom_call_target="tpu_custom_call" | custom-call | flops 805306368 | bytes 5000000 | tf_op jit(solution)/shard_map/pallas_call | solution.py:298
  4.9 10.2 %all-to-all-start = ((bf16[32,48,128]{2,1,0:T(8,128)(2,1)}), bf16[32,48,128]{2,1,0:T(8,128)(2,1)S(1)}, u32[]{:S(2)}, u32[]{:S(2)}) async-start(bf16[32,48,128]{2,1,0:T(8,128)(2,1)} %bitcast.21), calls=%async_computation | async-start | bytes 786432 | tf_op jit(solution)/shard_map/all_to_all | solution.py:317
  16.3 13.6 %all-to-all-done.part_ref = bf16[32,48,128]{2,1,0:T(8,128)(2,1)S(1)} async-done(((bf16[32,48,128]{2,1,0:T(8,128)(2,1)}), bf16[32,48,128]{2,1,0:T(8,128)(2,1)S(1)}, u32[]{:S(2)}, u32[]{:S(2)}) %all-to-all-start) | async-done | bytes 393248 | tf_op jit(solution)/shard_map/all_to_all | solution.py:317
  29.9 0.0 copy-done.1
  29.9 1.2 %shard_map.105 = f32[16,2,8,128]{3,2,1,0:T(8,128)} custom-call(s32[8,32]{1,0:T(8,128)S(1)} %broadcast_in_dim.18.owner_ref, bf16[32,48,128]{2,1,0:T(8,128)(2,1)S(1)} %all-to-all-done.part_ref), custom_call_target="tpu_custom_call" | custom-call | flops 1000000 | bytes 1000000 | tf_op jit(solution)/shard_map/pallas_call | solution.py:278
  31.1 11.9 %all-to-all-start.1 = ((f32[32,8,128]{2,1,0:T(8,128)}), f32[32,8,128]{2,1,0:T(8,128)S(1)}, u32[]{:S(2)}, u32[]{:S(2)}) async-start(f32[32,8,128]{2,1,0:T(8,128)} %bitcast.7), calls=%async_computation.1 | async-start | bytes 262144 | tf_op jit(solution)/shard_map/all_to_all | solution.py:330
  43.0 0.0 copy-done
  43.1 1.0 %bitcast_select_fusion.rows_ref = bf16[256,256]{1,0:T(8,128)(2,1)S(1)} fusion(bf16[16,256,256]{2,1,0:T(8,128)(2,1)} %constant.43.clone, s32[]{:T(128)S(6)} %select_n.20, pred[256]{0:T(512)(128)(4,1)S(1)} %compare_and_fusion), kind=kLoop, calls=%fused_computation | loop fusion | flops 65536 | bytes 262404 | tf_op jit(solution)/shard_map/jit(_where)/select_n | solution.py:339
  44.1 8.1 %all-to-all-done.1 = f32[32,8,128]{2,1,0:T(8,128)S(1)} async-done(((f32[32,8,128]{2,1,0:T(8,128)}), f32[32,8,128]{2,1,0:T(8,128)S(1)}, u32[]{:S(2)}, u32[]{:S(2)}) %all-to-all-start.1) | async-done | bytes 131104 | tf_op jit(solution)/shard_map/all_to_all | solution.py:330
  52.2 0.1 iota.17.keep_ref
  52.3 1.6 %shard_map.106 = (f32[32,8,128]{2,1,0:T(8,128)S(1)}, f32[448,128]{1,0:T(8,128)S(1)}) custom-call(f32[48,128]{1,0:T(8,128)S(1)} %iota.17.keep_ref, f32[256,128]{1,0:T(8,128)S(1)} %bitcast.19, bf16[256,256]{1,0:T(8,128)(2,1)S(1)} %bitcast_select_fusion.rows_ref, bf16[64,1024]{1,0:T(8,128)(2,1)S(1)} %pad.4.target_ref), custom_call_target="tpu_custom_call" | custom-call | flops 1000000 | bytes 1000000 | tf_op jit(solution)/shard_map/pallas_call | solution.py:278
  53.9 14.2 %all_to_all.15.gram_ref = f32[32,8,128]{2,1,0:T(8,128)S(1)} all-to-all(f32[32,8,128]{2,1,0:T(8,128)S(1)} %get-tuple-element.4), channel_id=1, replica_groups=mesh['freq'=16,'pair'=16,'half'=2] {'pair','half'}, dimensions={0} | all-to-all | bytes 262144 | tf_op jit(solution)/shard_map/all_to_all | solution.py:349
  68.2 2.6 %shard_map.107 = (bf16[48,8,128]{2,1,0:T(8,128)(2,1)}, f32[1,27]{1,0:T(1,128)}) custom-call(f32[48,128]{1,0:T(8,128)S(1)} %iota.17.keep_ref, f32[32,8,128]{2,1,0:T(8,128)S(1)} %all_to_all.15.gram_ref, f32[448,128]{1,0:T(8,128)S(1)} %get-tuple-element.5.trace_ref, bf16[48,8,128]{2,1,0:T(8,128)(2,1)S(1)} %copy-done), custom_call_target="tpu_custom_call" | custom-call | flops 1000000 | bytes 1000000 | tf_op jit(solution)/shard_map/pallas_call | solution.py:278
  (5 shorter events, 0.0 us)
Async XLA Ops:
  0.6 29.3 %copy-start.1 = (s32[32]{0:T(128)S(1)}, s32[32]{0:T(128)}, u32[]{:S(2)}) copy-start(s32[32]{0:T(128)} %param.12) | copy-start | bytes 388
  0.6 42.4 %copy-start = (bf16[48,8,128]{2,1,0:T(8,128)(2,1)S(1)}, bf16[48,8,128]{2,1,0:T(8,128)(2,1)}, u32[]{:S(2)}) copy-start(bf16[48,8,128]{2,1,0:T(8,128)(2,1)} %recorded_ref.1) | copy-start | bytes 294916
  4.9 25.1 %all-to-all-start = ((bf16[32,48,128]{2,1,0:T(8,128)(2,1)}), bf16[32,48,128]{2,1,0:T(8,128)(2,1)S(1)}, u32[]{:S(2)}, u32[]{:S(2)}) async-start(bf16[32,48,128]{2,1,0:T(8,128)(2,1)} %bitcast.21), calls=%async_computation | async-start | bytes 786432 | tf_op jit(solution)/shard_map/all_to_all | solution.py:317
  31.1 21.1 %all-to-all-start.1 = ((f32[32,8,128]{2,1,0:T(8,128)}), f32[32,8,128]{2,1,0:T(8,128)S(1)}, u32[]{:S(2)}, u32[]{:S(2)}) async-start(f32[32,8,128]{2,1,0:T(8,128)} %bitcast.7), calls=%async_computation.1 | async-start | bytes 262144 | tf_op jit(solution)/shard_map/all_to_all | solution.py:330

commit v7 on v6

--- a/solution.py
+++ b/solution.py
@@ -33,6 +33,7 @@
 IMAG_AT, SCALE_AT = HALF + 16, HALF + 32
 SPAN = 166.0
 VMEM = pl.BlockSpec(memory_space=pltpu.VMEM)
+ANY = pl.BlockSpec(memory_space=pl.ANY)
 F32 = jnp.float32
 BF16 = jnp.bfloat16
 
@@ -136,7 +137,8 @@
             out_ref[:, half, GAP_AT:] = tile.astype(BF16)
 
 
-def sum_and_fill(owner_ref, part_ref, out_ref, z_ref, w_ref, f_ref):
+def sum_and_fill(owner_ref, part_ref, keep_ref, rows_ref, target_ref, out_ref, z_ref, w_ref, f_ref):
+    del keep_ref, rows_ref, target_ref
     slots = part_ref.shape[0]
     total = jnp.zeros((16, RECV), F32)
     for j in range(slots):
@@ -315,20 +317,6 @@
     )(gap.T, recip_rows, data, weights)
     parts = parts.reshape(src_count, SLOT_ROWS, RECV)
     parts = lax.all_to_all(parts, ("pair", "half"), 0, 0, tiled=True)
-    copies = call(
-        sum_and_fill,
-        jax.ShapeDtypeStruct((NF, 2, 8, RECV), F32),
-        (jnp.broadcast_to(owner[None], (8, src_count)), parts),
-        [VMEM, VMEM],
-        [
-            pltpu.VMEM((NEAR * src_count, RECV), BF16),
-            pltpu.VMEM((NEAR * src_count, RECV), BF16),
-            pltpu.VMEM((RECV, RECV), F32),
-        ],
-    )
-    copies = copies.reshape(NF * 2, 8, RECV)
-    spread = lax.all_to_all(copies, ("freq", "half"), 0, 0, tiled=True).reshape(NF * 16, RECV)
-
     begin = freq_here * T_DEV - HALO
     first, last = start_row[0] - begin, end_row[0] - begin
     row = lax.broadcasted_iota(jnp.int32, (WROWS, RECV), 0)
@@ -338,6 +326,21 @@
     rows = lax.dynamic_index_in_dim(jnp.asarray(phase_rows()), freq_here, 0, keepdims=False)
     rows = jnp.where(keep[:, None], rows, jnp.zeros_like(rows))
     target = jnp.pad(recorded.reshape(WROWS, -1), ((0, 16), (0, 0)))
+
+    copies = call(
+        sum_and_fill,
+        jax.ShapeDtypeStruct((NF, 2, 8, RECV), F32),
+        (jnp.broadcast_to(owner[None], (8, src_count)), parts, keep_rows, rows, target),
+        [VMEM, VMEM, ANY, ANY, ANY],
+        [
+            pltpu.VMEM((NEAR * src_count, RECV), BF16),
+            pltpu.VMEM((NEAR * src_count, RECV), BF16),
+            pltpu.VMEM((RECV, RECV), F32),
+        ],
+    )
+    copies = copies.reshape(NF * 2, 8, RECV)
+    spread = lax.all_to_all(copies, ("freq", "half"), 0, 0, tiled=True).reshape(NF * 16, RECV)
+
     trace_rows = 8 * (WROWS + 2 * LEAD)
     gram, trace = call(
         trace_and_gram,

time: 71.1 us -> 70.2 us (0.987)
  blocking collectives: 14.2 us -> 35.2 us
  starting transfers between devices: 22.1 us -> 10.2 us
  waiting for transfers between devices: 21.7 us -> 12.5 us
    all_to_all x0 -> x1, blocking collectives: none -> 20.9 us  [body(): lax.all_to_all(copies, ('freq', 'half'), 0, 0, tiled=True)]
    all_to_all x1 -> x0, starting transfers between devices: 11.9 us -> none  [body(): lax.all_to_all(copies, ('freq', 'half'), 0, 0, tiled=True)]
    all_to_all x1 -> x0, waiting for transfers between devices: 8.11 us -> none  [body(): lax.all_to_all(copies, ('freq', 'half'), 0, 0, tiled=True)]
    all_to_all x1, waiting for transfers between devices: 13.6 us -> 12.5 us  [body(): parts = lax.all_to_all(parts, ('pair', 'half'), 0, 0, tiled=True)]
  transfers between devices with their start and end apart: 2 -> 1, of which waited for: 2 -> 1; matrix products, arithmetic and copies ran while one was open for 1% -> 2% of each run, Pallas kernels for 0% -> 0%
where the time goes in v7:
time: 70.2 us; the launch traced here: 69.9 us
  blocking collectives  35.2 us (50%)
  waiting for transfers between devices  12.5 us (18%)
  starting transfers between devices  10.2 us (15%)
  Pallas kernels  8.94 us (13%)
  between operations  2.02 us (3%)
  other arithmetic  1.02 us (1%)
    all_to_all x1, blocking collectives, body(): lax.all_to_all(copies, ('freq', 'half'), 0, 0, tiled=True)  20.9 us
    all_to_all x1, blocking collectives, body(): gram = lax.all_to_all(gram, ('pair', 'half'), 0, 0, tiled=True)  14.2 us
    all_to_all x1, waiting for transfers between devices, body(): parts = lax.all_to_all(parts, ('pair', 'half'), 0, 0, tiled=True)  12.5 us
    all_to_all x1, starting transfers between devices, body(): parts = lax.all_to_all(parts, ('pair', 'half'), 0, 0, tiled=True)  10.2 us
    pallas_call x3, Pallas kernels, call(): pl.pallas_call(kernel, out_shape=out_shape, in_specs=specs, out_specs=jax...  4.74 us
    pallas_call x1, Pallas kernels, body(): pl.pallas_call(main_product, grid=(points // depth,), out_shape=jax.Shape...  4.2 us
  transfers between devices with their start and end apart: 1, of which 1 were waited for; matrix products, arithmetic and copies ran while one was open for 2% of the time, Pallas kernels for 0%

profile of v7, /device:TPU:8, one launch (start us, length us, event | category | flops | bytes accessed | tf_op | source)
XLA Modules:
  0.0 69.9 jit_solution(13986285584286011610)
XLA Ops:
  0.6 0.0 copy-start
  0.6 0.0 copy-start.1
  0.7 4.2 %shard_map.104 = bf16[16,2,48,128]{3,2,1,0:T(8,128)(2,1)} custom-call(s32[16,128]{1,0:T(8,128)} %bitcast.24, bf16[32,128]{1,0:T(8,128)(2,1)} %bitcast.25, bf16[2,1,128,3072]{3,2,1,0:T(8,128)(2,1)} %data_ref.1, bf16[2,1,3072,256]{3,2,1,0:T(8,128)(2,1)} %weights_ref.1), custom_call_target="tpu_custom_call" | custom-call | flops 805306368 | bytes 5000000 | tf_op jit(solution)/shard_map/pallas_call | solution.py:300
  4.9 10.2 %all-to-all-start = ((bf16[32,48,128]{2,1,0:T(8,128)(2,1)}), bf16[32,48,128]{2,1,0:T(8,128)(2,1)S(1)}, u32[]{:S(2)}, u32[]{:S(2)}) async-start(bf16[32,48,128]{2,1,0:T(8,128)(2,1)} %bitcast.22), calls=%async_computation | async-start | bytes 786432 | tf_op jit(solution)/shard_map/all_to_all | solution.py:319
  16.3 0.0 copy-done
  16.4 1.0 %bitcast_select_fusion.rows_ref = bf16[256,256]{1,0:T(8,128)(2,1)S(1)} fusion(bf16[16,256,256]{2,1,0:T(8,128)(2,1)} %constant.43.clone, s32[]{:T(128)S(6)} %select_n.20, pred[256]{0:T(512)(128)(4,1)S(1)} %compare_and_fusion), kind=kLoop, calls=%fused_computation | loop fusion | flops 65536 | bytes 262404 | tf_op jit(solution)/shard_map/jit(_where)/select_n | solution.py:327
  17.4 12.5 %all-to-all-done.part_ref = bf16[32,48,128]{2,1,0:T(8,128)(2,1)S(1)} async-done(((bf16[32,48,128]{2,1,0:T(8,128)(2,1)}), bf16[32,48,128]{2,1,0:T(8,128)(2,1)S(1)}, u32[]{:S(2)}, u32[]{:S(2)}) %all-to-all-start) | async-done | bytes 393248 | tf_op jit(solution)/shard_map/all_to_all | solution.py:319
  29.9 0.1 iota.17.keep_ref
  30.0 0.0 copy-done.1
  30.0 0.5 shard_map.105
  30.5 20.9 %all_to_all.15 = f32[32,8,128]{2,1,0:T(8,128)S(1)} all-to-all(f32[32,8,128]{2,1,0:T(8,128)S(1)} %bitcast.20), channel_id=1, replica_groups=mesh['freq'=16,'pair'=16,'half'=2] {'freq','half'}, dimensions={0} | all-to-all | bytes 262144 | tf_op jit(solution)/shard_map/all_to_all | solution.py:342
  51.4 1.6 %shard_map.106 = (f32[32,8,128]{2,1,0:T(8,128)S(1)}, f32[448,128]{1,0:T(8,128)S(1)}) custom-call(f32[48,128]{1,0:T(8,128)S(1)} %iota.17.keep_ref, f32[256,128]{1,0:T(8,128)S(1)} %bitcast.19, bf16[256,256]{1,0:T(8,128)(2,1)S(1)} %bitcast_select_fusion.rows_ref, bf16[64,1024]{1,0:T(8,128)(2,1)S(1)} %pad.4.target_ref), custom_call_target="tpu_custom_call" | custom-call | flops 1000000 | bytes 1000000 | tf_op jit(solution)/shard_map/pallas_call | solution.py:280
  53.1 14.2 %all_to_all.16.gram_ref = f32[32,8,128]{2,1,0:T(8,128)S(1)} all-to-all(f32[32,8,128]{2,1,0:T(8,128)S(1)} %get-tuple-element.4), channel_id=1, replica_groups=mesh['freq'=16,'pair'=16,'half'=2] {'pair','half'}, dimensions={0} | all-to-all | bytes 262144 | tf_op jit(solution)/shard_map/all_to_all | solution.py:352
  67.3 2.6 %shard_map.107 = (bf16[48,8,128]{2,1,0:T(8,128)(2,1)}, f32[1,27]{1,0:T(1,128)}) custom-call(f32[48,128]{1,0:T(8,128)S(1)} %iota.17.keep_ref, f32[32,8,128]{2,1,0:T(8,128)S(1)} %all_to_all.16.gram_ref, f32[448,128]{1,0:T(8,128)S(1)} %get-tuple-element.5.trace_ref, bf16[48,8,128]{2,1,0:T(8,128)(2,1)S(1)} %copy-done), custom_call_target="tpu_custom_call" | custom-call | flops 1000000 | bytes 1000000 | tf_op jit(solution)/shard_map/pallas_call | solution.py:280
  (5 shorter events, 0.0 us)
Async XLA Ops:
  0.6 15.7 %copy-start = (bf16[48,8,128]{2,1,0:T(8,128)(2,1)S(1)}, bf16[48,8,128]{2,1,0:T(8,128)(2,1)}, u32[]{:S(2)}) copy-start(bf16[48,8,128]{2,1,0:T(8,128)(2,1)} %recorded_ref.1) | copy-start | bytes 294916
  0.6 29.3 %copy-start.1 = (s32[32]{0:T(128)S(1)}, s32[32]{0:T(128)}, u32[]{:S(2)}) copy-start(s32[32]{0:T(128)} %param.12) | copy-start | bytes 388
  4.9 25.1 %all-to-all-start = ((bf16[32,48,128]{2,1,0:T(8,128)(2,1)}), bf16[32,48,128]{2,1,0:T(8,128)(2,1)S(1)}, u32[]{:S(2)}, u32[]{:S(2)}) async-start(bf16[32,48,128]{2,1,0:T(8,128)(2,1)} %bitcast.22), calls=%async_computation | async-start | bytes 786432 | tf_op jit(solution)/shard_map/all_to_all | solution.py:319

commit v8 on v7

--- a/solution.py
+++ b/solution.py
@@ -180,24 +180,15 @@
     low = (rest - mid.astype(F32)).astype(BF16)
     stack = jnp.concatenate([high, mid, high, low, high, mid, target_ref[...]], axis=0)
     base = jnp.dot(rows_ref[...], stack, preferred_element_type=F32)
-    lag = lax.rem(lax.broadcasted_iota(jnp.int32, (GROWS, RECV), 0), GROUP)
-    recv = lax.broadcasted_iota(jnp.int32, (GROWS, RECV), 1)
-    ahead = (lag == 0) & (recv < RECV - 1)
-    behind = (lag == 2) & (recv > 0)
-    same = (lag == 1) | (lag == 3)
+    times = GROWS // GROUP
+    recv = lax.broadcasted_iota(jnp.int32, (times, RECV), 1)
     for s in range(sources):
-        at = slice(s * RECV, (s + 1) * RECV)
-        here = base[:, at]
-        shifted = jnp.where(
-            same,
-            here,
-            jnp.where(
-                ahead,
-                pltpu.roll(here, RECV - 1, 1),
-                jnp.where(behind, pltpu.roll(here, 1, 1), 0.0),
-            ),
-        )
-        a_ref[s * GROWS : (s + 1) * GROWS, :] = shifted
+        a_ref[s * GROWS : (s + 1) * GROWS, :] = base[:, s * RECV : (s + 1) * RECV]
+    for s in range(sources):
+        ahead = pl.ds(s * GROWS, times, stride=GROUP)
+        a_ref[ahead, :] = jnp.where(recv < RECV - 1, pltpu.roll(a_ref[ahead, :], RECV - 1, 1), 0.0)
+        behind = pl.ds(s * GROWS + 2, times, stride=GROUP)
+        a_ref[behind, :] = jnp.where(recv > 0, pltpu.roll(a_ref[behind, :], 1, 1), 0.0)
     for s in range(sources):
         mine = a_ref[pl.ds(s * GROWS + 1, WROWS + 2 * LEAD, stride=GROUP), :]
         trace_ref[pl.ds(s, WROWS + 2 * LEAD, stride=sources), :] = mine

time: 70.2 us -> 69.9 us (level)
  no operation moved by 1% of the time
where the time goes in v8:
time: 69.9 us; the launch traced here: 69.6 us
  blocking collectives  35.2 us (50%)
  waiting for transfers between devices  12.5 us (18%)
  starting transfers between devices  10.2 us (15%)
  Pallas kernels  8.61 us (12%)
  between operations  2.02 us (3%)
  other arithmetic  1.02 us (1%)
    all_to_all x1, blocking collectives, body(): lax.all_to_all(copies, ('freq', 'half'), 0, 0, tiled=True)  20.9 us
    all_to_all x1, blocking collectives, body(): gram = lax.all_to_all(gram, ('pair', 'half'), 0, 0, tiled=True)  14.2 us
    all_to_all x1, waiting for transfers between devices, body(): parts = lax.all_to_all(parts, ('pair', 'half'), 0, 0, tiled=True)  12.5 us
    all_to_all x1, starting transfers between devices, body(): parts = lax.all_to_all(parts, ('pair', 'half'), 0, 0, tiled=True)  10.2 us
    pallas_call x3, Pallas kernels, call(): pl.pallas_call(kernel, out_shape=out_shape, in_specs=specs, out_specs=jax...  4.41 us
    pallas_call x1, Pallas kernels, body(): pl.pallas_call(main_product, grid=(points // depth,), out_shape=jax.Shape...  4.2 us
  transfers between devices with their start and end apart: 1, of which 1 were waited for; matrix products, arithmetic and copies ran while one was open for 2% of the time, Pallas kernels for 0%

profile of v8, /device:TPU:8, one launch (start us, length us, event | category | flops | bytes accessed | tf_op | source)
XLA Modules:
  0.0 69.6 jit_solution(7713113712854444948)
XLA Ops:
  0.6 0.0 copy-start
  0.6 0.0 copy-start.1
  0.7 4.2 %shard_map.104 = bf16[16,2,48,128]{3,2,1,0:T(8,128)(2,1)} custom-call(s32[16,128]{1,0:T(8,128)} %bitcast.24, bf16[32,128]{1,0:T(8,128)(2,1)} %bitcast.25, bf16[2,1,128,3072]{3,2,1,0:T(8,128)(2,1)} %data_ref.1, bf16[2,1,3072,256]{3,2,1,0:T(8,128)(2,1)} %weights_ref.1), custom_call_target="tpu_custom_call" | custom-call | flops 805306368 | bytes 5000000 | tf_op jit(solution)/shard_map/pallas_call | solution.py:291
  4.9 10.2 %all-to-all-start = ((bf16[32,48,128]{2,1,0:T(8,128)(2,1)}), bf16[32,48,128]{2,1,0:T(8,128)(2,1)S(1)}, u32[]{:S(2)}, u32[]{:S(2)}) async-start(bf16[32,48,128]{2,1,0:T(8,128)(2,1)} %bitcast.22), calls=%async_computation | async-start | bytes 786432 | tf_op jit(solution)/shard_map/all_to_all | solution.py:310
  16.3 0.0 copy-done
  16.4 1.0 %bitcast_select_fusion.rows_ref = bf16[256,256]{1,0:T(8,128)(2,1)S(1)} fusion(bf16[16,256,256]{2,1,0:T(8,128)(2,1)} %constant.43.clone, s32[]{:T(128)S(6)} %select_n.20, pred[256]{0:T(512)(128)(4,1)S(1)} %compare_and_fusion), kind=kLoop, calls=%fused_computation | loop fusion | flops 65536 | bytes 262404 | tf_op jit(solution)/shard_map/jit(_where)/select_n | solution.py:318
  17.4 12.5 %all-to-all-done.part_ref = bf16[32,48,128]{2,1,0:T(8,128)(2,1)S(1)} async-done(((bf16[32,48,128]{2,1,0:T(8,128)(2,1)}), bf16[32,48,128]{2,1,0:T(8,128)(2,1)S(1)}, u32[]{:S(2)}, u32[]{:S(2)}) %all-to-all-start) | async-done | bytes 393248 | tf_op jit(solution)/shard_map/all_to_all | solution.py:310
  29.9 0.1 iota.17.keep_ref
  30.0 0.0 copy-done.1
  30.0 0.5 shard_map.105
  30.5 20.9 %all_to_all.15 = f32[32,8,128]{2,1,0:T(8,128)S(1)} all-to-all(f32[32,8,128]{2,1,0:T(8,128)S(1)} %bitcast.20), channel_id=1, replica_groups=mesh['freq'=16,'pair'=16,'half'=2] {'freq','half'}, dimensions={0} | all-to-all | bytes 262144 | tf_op jit(solution)/shard_map/all_to_all | solution.py:333
  51.4 1.3 %shard_map.106 = (f32[32,8,128]{2,1,0:T(8,128)S(1)}, f32[448,128]{1,0:T(8,128)S(1)}) custom-call(f32[48,128]{1,0:T(8,128)S(1)} %iota.17.keep_ref, f32[256,128]{1,0:T(8,128)S(1)} %bitcast.19, bf16[256,256]{1,0:T(8,128)(2,1)S(1)} %bitcast_select_fusion.rows_ref, bf16[64,1024]{1,0:T(8,128)(2,1)S(1)} %pad.4.target_ref), custom_call_target="tpu_custom_call" | custom-call | flops 1000000 | bytes 1000000 | tf_op jit(solution)/shard_map/pallas_call | solution.py:271
  52.7 14.2 %all_to_all.16.gram_ref = f32[32,8,128]{2,1,0:T(8,128)S(1)} all-to-all(f32[32,8,128]{2,1,0:T(8,128)S(1)} %get-tuple-element.4), channel_id=1, replica_groups=mesh['freq'=16,'pair'=16,'half'=2] {'pair','half'}, dimensions={0} | all-to-all | bytes 262144 | tf_op jit(solution)/shard_map/all_to_all | solution.py:343
  67.0 2.6 %shard_map.107 = (bf16[48,8,128]{2,1,0:T(8,128)(2,1)}, f32[1,27]{1,0:T(1,128)}) custom-call(f32[48,128]{1,0:T(8,128)S(1)} %iota.17.keep_ref, f32[32,8,128]{2,1,0:T(8,128)S(1)} %all_to_all.16.gram_ref, f32[448,128]{1,0:T(8,128)S(1)} %get-tuple-element.5.trace_ref, bf16[48,8,128]{2,1,0:T(8,128)(2,1)S(1)} %copy-done), custom_call_target="tpu_custom_call" | custom-call | flops 1000000 | bytes 1000000 | tf_op jit(solution)/shard_map/pallas_call | solution.py:271
  (5 shorter events, 0.0 us)
Async XLA Ops:
  0.6 15.7 %copy-start = (bf16[48,8,128]{2,1,0:T(8,128)(2,1)S(1)}, bf16[48,8,128]{2,1,0:T(8,128)(2,1)}, u32[]{:S(2)}) copy-start(bf16[48,8,128]{2,1,0:T(8,128)(2,1)} %recorded_ref.1) | copy-start | bytes 294916
  0.6 29.3 %copy-start.1 = (s32[32]{0:T(128)S(1)}, s32[32]{0:T(128)}, u32[]{:S(2)}) copy-start(s32[32]{0:T(128)} %param.12) | copy-start | bytes 388
  4.9 25.1 %all-to-all-start = ((bf16[32,48,128]{2,1,0:T(8,128)(2,1)}), bf16[32,48,128]{2,1,0:T(8,128)(2,1)S(1)}, u32[]{:S(2)}, u32[]{:S(2)}) async-start(bf16[32,48,128]{2,1,0:T(8,128)(2,1)} %bitcast.22), calls=%async_computation | async-start | bytes 786432 | tf_op jit(solution)/shard_map/all_to_all | solution.py:310

commit v9 on v8

--- a/solution.py
+++ b/solution.py
@@ -194,9 +194,9 @@
         trace_ref[pl.ds(s, WROWS + 2 * LEAD, stride=sources), :] = mine
     high, low = two_parts(jnp.concatenate([a_ref[s * GROWS : (s + 1) * GROWS, :] for s in range(sources)], axis=1))
     dims = (((1,), (1,)), ((), ()))
-    g_ref[...] = lax.dot_general(high, high, dims, preferred_element_type=F32) + 2.0 * lax.dot_general(
-        high, low, dims, preferred_element_type=F32
-    )
+    left = jnp.concatenate([high, high, low], axis=1)
+    right = jnp.concatenate([high, 2.0 * low, low], axis=1)
+    g_ref[...] = lax.dot_general(left, right, dims, preferred_element_type=F32)
     total = jnp.zeros((SIDE, RECV), F32)
     for u in range(WROWS):
         at = GROUP * u

time: 69.9 us -> 70.1 us (level)
  no operation moved by 1% of the time
where the time goes in v9:
time: 70.1 us; the launch traced here: 69.9 us
  blocking collectives  35.2 us (50%)
  waiting for transfers between devices  12.5 us (18%)
  starting transfers between devices  10.2 us (15%)
  Pallas kernels  8.89 us (13%)
  between operations  2.02 us (3%)
  other arithmetic  1.02 us (1%)
    all_to_all x1, blocking collectives, body(): lax.all_to_all(copies, ('freq', 'half'), 0, 0, tiled=True)  20.9 us
    all_to_all x1, blocking collectives, body(): gram = lax.all_to_all(gram, ('pair', 'half'), 0, 0, tiled=True)  14.2 us
    all_to_all x1, waiting for transfers between devices, body(): parts = lax.all_to_all(parts, ('pair', 'half'), 0, 0, tiled=True)  12.5 us
    all_to_all x1, starting transfers between devices, body(): parts = lax.all_to_all(parts, ('pair', 'half'), 0, 0, tiled=True)  10.2 us
    pallas_call x3, Pallas kernels, call(): pl.pallas_call(kernel, out_shape=out_shape, in_specs=specs, out_specs=jax...  4.69 us
    pallas_call x1, Pallas kernels, body(): pl.pallas_call(main_product, grid=(points // depth,), out_shape=jax.Shape...  4.2 us
  transfers between devices with their start and end apart: 1, of which 1 were waited for; matrix products, arithmetic and copies ran while one was open for 2% of the time, Pallas kernels for 0%

profile of v9, /device:TPU:8, one launch (start us, length us, event | category | flops | bytes accessed | tf_op | source)
XLA Modules:
  0.0 69.9 jit_solution(6613513087267485976)
XLA Ops:
  0.6 0.0 copy-start
  0.6 0.0 copy-start.1
  0.7 4.2 %shard_map.104 = bf16[16,2,48,128]{3,2,1,0:T(8,128)(2,1)} custom-call(s32[16,128]{1,0:T(8,128)} %bitcast.24, bf16[32,128]{1,0:T(8,128)(2,1)} %bitcast.25, bf16[2,1,128,3072]{3,2,1,0:T(8,128)(2,1)} %data_ref.1, bf16[2,1,3072,256]{3,2,1,0:T(8,128)(2,1)} %weights_ref.1), custom_call_target="tpu_custom_call" | custom-call | flops 805306368 | bytes 5000000 | tf_op jit(solution)/shard_map/pallas_call | solution.py:291
  4.9 10.2 %all-to-all-start = ((bf16[32,48,128]{2,1,0:T(8,128)(2,1)}), bf16[32,48,128]{2,1,0:T(8,128)(2,1)S(1)}, u32[]{:S(2)}, u32[]{:S(2)}) async-start(bf16[32,48,128]{2,1,0:T(8,128)(2,1)} %bitcast.22), calls=%async_computation | async-start | bytes 786432 | tf_op jit(solution)/shard_map/all_to_all | solution.py:310
  16.3 0.0 copy-done
  16.4 1.0 %bitcast_select_fusion.rows_ref = bf16[256,256]{1,0:T(8,128)(2,1)S(1)} fusion(bf16[16,256,256]{2,1,0:T(8,128)(2,1)} %constant.43.clone, s32[]{:T(128)S(6)} %select_n.20, pred[256]{0:T(512)(128)(4,1)S(1)} %compare_and_fusion), kind=kLoop, calls=%fused_computation | loop fusion | flops 65536 | bytes 262404 | tf_op jit(solution)/shard_map/jit(_where)/select_n | solution.py:318
  17.4 12.5 %all-to-all-done.part_ref = bf16[32,48,128]{2,1,0:T(8,128)(2,1)S(1)} async-done(((bf16[32,48,128]{2,1,0:T(8,128)(2,1)}), bf16[32,48,128]{2,1,0:T(8,128)(2,1)S(1)}, u32[]{:S(2)}, u32[]{:S(2)}) %all-to-all-start) | async-done | bytes 393248 | tf_op jit(solution)/shard_map/all_to_all | solution.py:310
  29.9 0.1 iota.17.keep_ref
  30.0 0.0 copy-done.1
  30.0 0.5 shard_map.105
  30.5 20.9 %all_to_all.15 = f32[32,8,128]{2,1,0:T(8,128)S(1)} all-to-all(f32[32,8,128]{2,1,0:T(8,128)S(1)} %bitcast.20), channel_id=1, replica_groups=mesh['freq'=16,'pair'=16,'half'=2] {'freq','half'}, dimensions={0} | all-to-all | bytes 262144 | tf_op jit(solution)/shard_map/all_to_all | solution.py:333
  51.4 1.6 %shard_map.106 = (f32[32,8,128]{2,1,0:T(8,128)S(1)}, f32[448,128]{1,0:T(8,128)S(1)}) custom-call(f32[48,128]{1,0:T(8,128)S(1)} %iota.17.keep_ref, f32[256,128]{1,0:T(8,128)S(1)} %bitcast.19, bf16[256,256]{1,0:T(8,128)(2,1)S(1)} %bitcast_select_fusion.rows_ref, bf16[64,1024]{1,0:T(8,128)(2,1)S(1)} %pad.4.target_ref), custom_call_target="tpu_custom_call" | custom-call | flops 1000000 | bytes 1000000 | tf_op jit(solution)/shard_map/pallas_call | solution.py:271
  53.0 14.2 %all_to_all.16.gram_ref = f32[32,8,128]{2,1,0:T(8,128)S(1)} all-to-all(f32[32,8,128]{2,1,0:T(8,128)S(1)} %get-tuple-element.4), channel_id=1, replica_groups=mesh['freq'=16,'pair'=16,'half'=2] {'pair','half'}, dimensions={0} | all-to-all | bytes 262144 | tf_op jit(solution)/shard_map/all_to_all | solution.py:343
  67.3 2.6 %shard_map.107 = (bf16[48,8,128]{2,1,0:T(8,128)(2,1)}, f32[1,27]{1,0:T(1,128)}) custom-call(f32[48,128]{1,0:T(8,128)S(1)} %iota.17.keep_ref, f32[32,8,128]{2,1,0:T(8,128)S(1)} %all_to_all.16.gram_ref, f32[448,128]{1,0:T(8,128)S(1)} %get-tuple-element.5.trace_ref, bf16[48,8,128]{2,1,0:T(8,128)(2,1)S(1)} %copy-done), custom_call_target="tpu_custom_call" | custom-call | flops 1000000 | bytes 1000000 | tf_op jit(solution)/shard_map/pallas_call | solution.py:271
  (5 shorter events, 0.0 us)
Async XLA Ops:
  0.6 15.7 %copy-start = (bf16[48,8,128]{2,1,0:T(8,128)(2,1)S(1)}, bf16[48,8,128]{2,1,0:T(8,128)(2,1)}, u32[]{:S(2)}) copy-start(bf16[48,8,128]{2,1,0:T(8,128)(2,1)} %recorded_ref.1) | copy-start | bytes 294916
  0.6 29.3 %copy-start.1 = (s32[32]{0:T(128)S(1)}, s32[32]{0:T(128)}, u32[]{:S(2)}) copy-start(s32[32]{0:T(128)} %param.12) | copy-start | bytes 388
  4.9 25.1 %all-to-all-start = ((bf16[32,48,128]{2,1,0:T(8,128)(2,1)}), bf16[32,48,128]{2,1,0:T(8,128)(2,1)S(1)}, u32[]{:S(2)}, u32[]{:S(2)}) async-start(bf16[32,48,128]{2,1,0:T(8,128)(2,1)} %bitcast.22), calls=%async_computation | async-start | bytes 786432 | tf_op jit(solution)/shard_map/all_to_all | solution.py:310

commit v10 on v8

--- a/solution.py
+++ b/solution.py
@@ -23,6 +23,7 @@
 NF = 16
 GROUP = 4
 GROWS = 256
+AROWS = GROUP * (WROWS + 2 * LEAD)
 SIDE = 40
 UNKNOWNS = LAGS_T * LAGS_X
 TARGET_COL = GROUP * LEAD + 3
@@ -48,7 +49,7 @@
 
 @functools.cache
 def phase_rows():
-    table = np.zeros((NF, GROWS, 256), ml_dtypes.bfloat16)
+    table = np.zeros((NF, AROWS, 256), ml_dtypes.bfloat16)
     freqs = np.arange(NF)
     scale = 1.0 / math.sqrt(NF)
     for window in range(NF):
@@ -180,23 +181,26 @@
     low = (rest - mid.astype(F32)).astype(BF16)
     stack = jnp.concatenate([high, mid, high, low, high, mid, target_ref[...]], axis=0)
     base = jnp.dot(rows_ref[...], stack, preferred_element_type=F32)
-    times = GROWS // GROUP
+    times = AROWS // GROUP
     recv = lax.broadcasted_iota(jnp.int32, (times, RECV), 1)
     for s in range(sources):
-        a_ref[s * GROWS : (s + 1) * GROWS, :] = base[:, s * RECV : (s + 1) * RECV]
+        a_ref[s * AROWS : (s + 1) * AROWS, :] = base[:, s * RECV : (s + 1) * RECV]
     for s in range(sources):
-        ahead = pl.ds(s * GROWS, times, stride=GROUP)
+        ahead = pl.ds(s * AROWS, times, stride=GROUP)
         a_ref[ahead, :] = jnp.where(recv < RECV - 1, pltpu.roll(a_ref[ahead, :], RECV - 1, 1), 0.0)
-        behind = pl.ds(s * GROWS + 2, times, stride=GROUP)
+        behind = pl.ds(s * AROWS + 2, times, stride=GROUP)
         a_ref[behind, :] = jnp.where(recv > 0, pltpu.roll(a_ref[behind, :], 1, 1), 0.0)
     for s in range(sources):
-        mine = a_ref[pl.ds(s * GROWS + 1, WROWS + 2 * LEAD, stride=GROUP), :]
+        mine = a_ref[pl.ds(s * AROWS + 1, WROWS + 2 * LEAD, stride=GROUP), :]
         trace_ref[pl.ds(s, WROWS + 2 * LEAD, stride=sources), :] = mine
-    high, low = two_parts(jnp.concatenate([a_ref[s * GROWS : (s + 1) * GROWS, :] for s in range(sources)], axis=1))
+    high, low = two_parts(jnp.concatenate([a_ref[s * AROWS : (s + 1) * AROWS, :] for s in range(sources)], axis=1))
     dims = (((1,), (1,)), ((), ()))
-    g_ref[...] = lax.dot_general(high, high, dims, preferred_element_type=F32) + 2.0 * lax.dot_general(
-        high, low, dims, preferred_element_type=F32
-    )
+    rest = jnp.zeros((GROWS - AROWS, high.shape[1]), BF16)
+    wide, narrow = (jnp.concatenate([part, rest], axis=0) for part in (high, low))
+    g_ref[:AROWS] = lax.dot_general(high, wide, dims, preferred_element_type=F32) + 2.0 * lax.dot_general(
+        high, narrow, dims, preferred_element_type=F32
+    )
+    g_ref[AROWS:] = jnp.zeros((GROWS - AROWS, GROWS), F32)
     total = jnp.zeros((SIDE, RECV), F32)
     for u in range(WROWS):
         at = GROUP * u
@@ -312,7 +316,7 @@
     first, last = start_row[0] - begin, end_row[0] - begin
     row = lax.broadcasted_iota(jnp.int32, (WROWS, RECV), 0)
     keep_rows = ((row >= first) & (row < last)).astype(F32)
-    row = jnp.arange(GROWS, dtype=jnp.int32) // GROUP - LEAD
+    row = jnp.arange(AROWS, dtype=jnp.int32) // GROUP - LEAD
     keep = (row >= first) & (row < last)
     rows = lax.dynamic_index_in_dim(jnp.asarray(phase_rows()), freq_here, 0, keepdims=False)
     rows = jnp.where(keep[:, None], rows, jnp.zeros_like(rows))
@@ -338,7 +342,7 @@
         (jax.ShapeDtypeStruct((src_count, 8, RECV), F32), jax.ShapeDtypeStruct((trace_rows, RECV), F32)),
         (keep_rows, spread, rows, target),
         [VMEM] * 4,
-        [pltpu.VMEM((8 * GROWS, RECV), F32), pltpu.VMEM((GROWS, GROWS), F32)],
+        [pltpu.VMEM((8 * AROWS, RECV), F32), pltpu.VMEM((GROWS, GROWS), F32)],
     )
     gram = lax.all_to_all(gram, ("pair", "half"), 0, 0, tiled=True)
     damping = float(WROWS * total_out * RECV)

time: 69.9 us -> 69.9 us (level)
  transfers between devices with their start and end apart: 1 -> 1, of which waited for: 1 -> 1; matrix products, arithmetic and copies ran while one was open for 2% -> 1% of each run, Pallas kernels for 0% -> 0%
where the time goes in v10:
time: 69.9 us; the launch traced here: 69.5 us
  blocking collectives  35.2 us (50%)
  waiting for transfers between devices  12.5 us (18%)
  starting transfers between devices  10.2 us (15%)
  Pallas kernels  8.56 us (12%)
  between operations  2.02 us (3%)
  other arithmetic  1.01 us (1%)
    all_to_all x1, blocking collectives, body(): lax.all_to_all(copies, ('freq', 'half'), 0, 0, tiled=True)  20.9 us
    all_to_all x1, blocking collectives, body(): gram = lax.all_to_all(gram, ('pair', 'half'), 0, 0, tiled=True)  14.2 us
    all_to_all x1, waiting for transfers between devices, body(): parts = lax.all_to_all(parts, ('pair', 'half'), 0, 0, tiled=True)  12.5 us
    all_to_all x1, starting transfers between devices, body(): parts = lax.all_to_all(parts, ('pair', 'half'), 0, 0, tiled=True)  10.2 us
    pallas_call x3, Pallas kernels, call(): pl.pallas_call(kernel, out_shape=out_shape, in_specs=specs, out_specs=jax...  4.36 us
    pallas_call x1, Pallas kernels, body(): pl.pallas_call(main_product, grid=(points // depth,), out_shape=jax.Shape...  4.2 us
  transfers between devices with their start and end apart: 1, of which 1 were waited for; matrix products, arithmetic and copies ran while one was open for 1% of the time, Pallas kernels for 0%

profile of v10, /device:TPU:8, one launch (start us, length us, event | category | flops | bytes accessed | tf_op | source)
XLA Modules:
  0.0 69.5 jit_solution(6657437151852299379)
XLA Ops:
  0.6 0.0 copy-start
  0.6 0.0 copy-start.1
  0.7 4.2 %shard_map.104 = bf16[16,2,48,128]{3,2,1,0:T(8,128)(2,1)} custom-call(s32[16,128]{1,0:T(8,128)} %bitcast.24, bf16[32,128]{1,0:T(8,128)(2,1)} %bitcast.25, bf16[2,1,128,3072]{3,2,1,0:T(8,128)(2,1)} %data_ref.1, bf16[2,1,3072,256]{3,2,1,0:T(8,128)(2,1)} %weights_ref.1), custom_call_target="tpu_custom_call" | custom-call | flops 805306368 | bytes 5000000 | tf_op jit(solution)/shard_map/pallas_call | solution.py:295
  4.9 10.2 %all-to-all-start = ((bf16[32,48,128]{2,1,0:T(8,128)(2,1)}), bf16[32,48,128]{2,1,0:T(8,128)(2,1)S(1)}, u32[]{:S(2)}, u32[]{:S(2)}) async-start(bf16[32,48,128]{2,1,0:T(8,128)(2,1)} %bitcast.22), calls=%async_computation | async-start | bytes 786432 | tf_op jit(solution)/shard_map/all_to_all | solution.py:314
  16.3 0.0 copy-done
  16.4 1.0 %bitcast_select_fusion.rows_ref = bf16[224,256]{1,0:T(8,128)(2,1)S(1)} fusion(bf16[16,224,256]{2,1,0:T(8,128)(2,1)} %constant.43.clone, s32[]{:T(128)S(6)} %select_n.20, pred[224]{0:T(512)(128)(4,1)S(1)} %compare_and_fusion), kind=kLoop, calls=%fused_computation | loop fusion | flops 57344 | bytes 229604 | tf_op jit(solution)/shard_map/jit(_where)/select_n | solution.py:322
  17.4 12.5 %all-to-all-done.part_ref = bf16[32,48,128]{2,1,0:T(8,128)(2,1)S(1)} async-done(((bf16[32,48,128]{2,1,0:T(8,128)(2,1)}), bf16[32,48,128]{2,1,0:T(8,128)(2,1)S(1)}, u32[]{:S(2)}, u32[]{:S(2)}) %all-to-all-start) | async-done | bytes 393248 | tf_op jit(solution)/shard_map/all_to_all | solution.py:314
  29.9 0.1 iota.17.keep_ref
  30.0 0.0 copy-done.1
  30.0 0.5 shard_map.105
  30.5 20.9 %all_to_all.15 = f32[32,8,128]{2,1,0:T(8,128)S(1)} all-to-all(f32[32,8,128]{2,1,0:T(8,128)S(1)} %bitcast.20), channel_id=1, replica_groups=mesh['freq'=16,'pair'=16,'half'=2] {'freq','half'}, dimensions={0} | all-to-all | bytes 262144 | tf_op jit(solution)/shard_map/all_to_all | solution.py:337
  51.4 1.3 %shard_map.106 = (f32[32,8,128]{2,1,0:T(8,128)S(1)}, f32[448,128]{1,0:T(8,128)S(1)}) custom-call(f32[48,128]{1,0:T(8,128)S(1)} %iota.17.keep_ref, f32[256,128]{1,0:T(8,128)S(1)} %bitcast.19, bf16[224,256]{1,0:T(8,128)(2,1)S(1)} %bitcast_select_fusion.rows_ref, bf16[64,1024]{1,0:T(8,128)(2,1)S(1)} %pad.4.target_ref), custom_call_target="tpu_custom_call" | custom-call | flops 1000000 | bytes 1000000 | tf_op jit(solution)/shard_map/pallas_call | solution.py:275
  52.7 14.2 %all_to_all.16.gram_ref = f32[32,8,128]{2,1,0:T(8,128)S(1)} all-to-all(f32[32,8,128]{2,1,0:T(8,128)S(1)} %get-tuple-element.4), channel_id=1, replica_groups=mesh['freq'=16,'pair'=16,'half'=2] {'pair','half'}, dimensions={0} | all-to-all | bytes 262144 | tf_op jit(solution)/shard_map/all_to_all | solution.py:347
  66.9 2.6 %shard_map.107 = (bf16[48,8,128]{2,1,0:T(8,128)(2,1)}, f32[1,27]{1,0:T(1,128)}) custom-call(f32[48,128]{1,0:T(8,128)S(1)} %iota.17.keep_ref, f32[32,8,128]{2,1,0:T(8,128)S(1)} %all_to_all.16.gram_ref, f32[448,128]{1,0:T(8,128)S(1)} %get-tuple-element.5.trace_ref, bf16[48,8,128]{2,1,0:T(8,128)(2,1)S(1)} %copy-done), custom_call_target="tpu_custom_call" | custom-call | flops 1000000 | bytes 1000000 | tf_op jit(solution)/shard_map/pallas_call | solution.py:275
  (5 shorter events, 0.0 us)
Async XLA Ops:
  0.6 15.7 %copy-start = (bf16[48,8,128]{2,1,0:T(8,128)(2,1)S(1)}, bf16[48,8,128]{2,1,0:T(8,128)(2,1)}, u32[]{:S(2)}) copy-start(bf16[48,8,128]{2,1,0:T(8,128)(2,1)} %recorded_ref.1) | copy-start | bytes 294916
  0.6 29.3 %copy-start.1 = (s32[32]{0:T(128)S(1)}, s32[32]{0:T(128)}, u32[]{:S(2)}) copy-start(s32[32]{0:T(128)} %param.12) | copy-start | bytes 388
  4.9 25.1 %all-to-all-start = ((bf16[32,48,128]{2,1,0:T(8,128)(2,1)}), bf16[32,48,128]{2,1,0:T(8,128)(2,1)S(1)}, u32[]{:S(2)}, u32[]{:S(2)}) async-start(bf16[32,48,128]{2,1,0:T(8,128)(2,1)} %bitcast.22), calls=%async_computation | async-start | bytes 786432 | tf_op jit(solution)/shard_map/all_to_all | solution.py:314

commit v11 on v10

--- a/solution.py
+++ b/solution.py
@@ -211,7 +211,9 @@
             part = g_ref[at : at + SIDE, RECV:]
             part = pltpu.roll(part, (2 * RECV - at) % RECV, 1)
         else:
-            part = pltpu.roll(g_ref[at : at + SIDE, :], 2 * RECV - at, 1)[:, :RECV]
+            lane = lax.broadcasted_iota(jnp.int32, (SIDE, RECV), 1)
+            part = jnp.where(lane >= at, g_ref[at : at + SIDE, :RECV], g_ref[at : at + SIDE, RECV:])
+            part = pltpu.roll(part, RECV - at, 1)
         total = total + part * keep_ref[u : u + 1, :]
     full = jnp.concatenate([total, jnp.zeros((RECV - SIDE, RECV), F32)], axis=0)
     total = 0.5 * (total + full.T[:SIDE])

time: 69.9 us -> 69.8 us (level)
  no operation moved by 1% of the time
where the time goes in v11:
time: 69.8 us; the launch traced here: 69.5 us
  blocking collectives  35.2 us (50%)
  waiting for transfers between devices  12.5 us (18%)
  starting transfers between devices  10.2 us (15%)
  Pallas kernels  8.53 us (12%)
  between operations  2.02 us (3%)
  other arithmetic  1.01 us (1%)
    all_to_all x1, blocking collectives, body(): lax.all_to_all(copies, ('freq', 'half'), 0, 0, tiled=True)  20.9 us
    all_to_all x1, blocking collectives, body(): gram = lax.all_to_all(gram, ('pair', 'half'), 0, 0, tiled=True)  14.2 us
    all_to_all x1, waiting for transfers between devices, body(): parts = lax.all_to_all(parts, ('pair', 'half'), 0, 0, tiled=True)  12.5 us
    all_to_all x1, starting transfers between devices, body(): parts = lax.all_to_all(parts, ('pair', 'half'), 0, 0, tiled=True)  10.2 us
    pallas_call x3, Pallas kernels, call(): pl.pallas_call(kernel, out_shape=out_shape, in_specs=specs, out_specs=jax...  4.33 us
    pallas_call x1, Pallas kernels, body(): pl.pallas_call(main_product, grid=(points // depth,), out_shape=jax.Shape...  4.2 us
  transfers between devices with their start and end apart: 1, of which 1 were waited for; matrix products, arithmetic and copies ran while one was open for 1% of the time, Pallas kernels for 0%

profile of v11, /device:TPU:8, one launch (start us, length us, event | category | flops | bytes accessed | tf_op | source)
XLA Modules:
  0.0 69.5 jit_solution(7570347859199063893)
XLA Ops:
  0.6 0.0 copy-start
  0.6 0.0 copy-start.1
  0.7 4.2 %shard_map.104 = bf16[16,2,48,128]{3,2,1,0:T(8,128)(2,1)} custom-call(s32[16,128]{1,0:T(8,128)} %bitcast.24, bf16[32,128]{1,0:T(8,128)(2,1)} %bitcast.25, bf16[2,1,128,3072]{3,2,1,0:T(8,128)(2,1)} %data_ref.1, bf16[2,1,3072,256]{3,2,1,0:T(8,128)(2,1)} %weights_ref.1), custom_call_target="tpu_custom_call" | custom-call | flops 805306368 | bytes 5000000 | tf_op jit(solution)/shard_map/pallas_call | solution.py:297
  4.9 10.2 %all-to-all-start = ((bf16[32,48,128]{2,1,0:T(8,128)(2,1)}), bf16[32,48,128]{2,1,0:T(8,128)(2,1)S(1)}, u32[]{:S(2)}, u32[]{:S(2)}) async-start(bf16[32,48,128]{2,1,0:T(8,128)(2,1)} %bitcast.22), calls=%async_computation | async-start | bytes 786432 | tf_op jit(solution)/shard_map/all_to_all | solution.py:316
  16.3 0.0 copy-done
  16.4 1.0 %bitcast_select_fusion.rows_ref = bf16[224,256]{1,0:T(8,128)(2,1)S(1)} fusion(bf16[16,224,256]{2,1,0:T(8,128)(2,1)} %constant.43.clone, s32[]{:T(128)S(6)} %select_n.20, pred[224]{0:T(512)(128)(4,1)S(1)} %compare_and_fusion), kind=kLoop, calls=%fused_computation | loop fusion | flops 57344 | bytes 229604 | tf_op jit(solution)/shard_map/jit(_where)/select_n | solution.py:324
  17.4 12.5 %all-to-all-done.part_ref = bf16[32,48,128]{2,1,0:T(8,128)(2,1)S(1)} async-done(((bf16[32,48,128]{2,1,0:T(8,128)(2,1)}), bf16[32,48,128]{2,1,0:T(8,128)(2,1)S(1)}, u32[]{:S(2)}, u32[]{:S(2)}) %all-to-all-start) | async-done | bytes 393248 | tf_op jit(solution)/shard_map/all_to_all | solution.py:316
  29.9 0.1 iota.17.keep_ref
  30.0 0.0 copy-done.1
  30.0 0.5 shard_map.105
  30.5 20.9 %all_to_all.15 = f32[32,8,128]{2,1,0:T(8,128)S(1)} all-to-all(f32[32,8,128]{2,1,0:T(8,128)S(1)} %bitcast.20), channel_id=1, replica_groups=mesh['freq'=16,'pair'=16,'half'=2] {'freq','half'}, dimensions={0} | all-to-all | bytes 262144 | tf_op jit(solution)/shard_map/all_to_all | solution.py:339
  51.4 1.2 %shard_map.106 = (f32[32,8,128]{2,1,0:T(8,128)S(1)}, f32[448,128]{1,0:T(8,128)S(1)}) custom-call(f32[48,128]{1,0:T(8,128)S(1)} %iota.17.keep_ref, f32[256,128]{1,0:T(8,128)S(1)} %bitcast.19, bf16[224,256]{1,0:T(8,128)(2,1)S(1)} %bitcast_select_fusion.rows_ref, bf16[64,1024]{1,0:T(8,128)(2,1)S(1)} %pad.4.target_ref), custom_call_target="tpu_custom_call" | custom-call | flops 1000000 | bytes 1000000 | tf_op jit(solution)/shard_map/pallas_call | solution.py:277
  52.7 14.2 %all_to_all.16.gram_ref = f32[32,8,128]{2,1,0:T(8,128)S(1)} all-to-all(f32[32,8,128]{2,1,0:T(8,128)S(1)} %get-tuple-element.4), channel_id=1, replica_groups=mesh['freq'=16,'pair'=16,'half'=2] {'pair','half'}, dimensions={0} | all-to-all | bytes 262144 | tf_op jit(solution)/shard_map/all_to_all | solution.py:349
  66.9 2.6 %shard_map.107 = (bf16[48,8,128]{2,1,0:T(8,128)(2,1)}, f32[1,27]{1,0:T(1,128)}) custom-call(f32[48,128]{1,0:T(8,128)S(1)} %iota.17.keep_ref, f32[32,8,128]{2,1,0:T(8,128)S(1)} %all_to_all.16.gram_ref, f32[448,128]{1,0:T(8,128)S(1)} %get-tuple-element.5.trace_ref, bf16[48,8,128]{2,1,0:T(8,128)(2,1)S(1)} %copy-done), custom_call_target="tpu_custom_call" | custom-call | flops 1000000 | bytes 1000000 | tf_op jit(solution)/shard_map/pallas_call | solution.py:277
  (5 shorter events, 0.0 us)
Async XLA Ops:
  0.6 15.7 %copy-start = (bf16[48,8,128]{2,1,0:T(8,128)(2,1)S(1)}, bf16[48,8,128]{2,1,0:T(8,128)(2,1)}, u32[]{:S(2)}) copy-start(bf16[48,8,128]{2,1,0:T(8,128)(2,1)} %recorded_ref.1) | copy-start | bytes 294916
  0.6 29.3 %copy-start.1 = (s32[32]{0:T(128)S(1)}, s32[32]{0:T(128)}, u32[]{:S(2)}) copy-start(s32[32]{0:T(128)} %param.12) | copy-start | bytes 388
  4.9 25.1 %all-to-all-start = ((bf16[32,48,128]{2,1,0:T(8,128)(2,1)}), bf16[32,48,128]{2,1,0:T(8,128)(2,1)S(1)}, u32[]{:S(2)}, u32[]{:S(2)}) async-start(bf16[32,48,128]{2,1,0:T(8,128)(2,1)} %bitcast.22), calls=%async_computation | async-start | bytes 786432 | tf_op jit(solution)/shard_map/all_to_all | solution.py:316
